TPU v7x, 32 devices: a whole 2x2x4 slice. The times are simulated.
32 devices in a mesh: section: 2 (over core), tok: 16 (over z, y, x).
Axes of the slice: x: 2, y: 2, z: 4, core: 2. Of those that a mesh axis runs over, the one named last changes fastest.
Arguments:
- tokens: bfloat16 [3, 128, 16, 32, 192], P(None, 'tok'), may hold values from -6 to 6
- cotangent: bfloat16 [3, 128, 16, 32, 192], P(None, 'tok'), may hold values from -6 to 6
- ln1_gain: bfloat16 [2, 192], P('section'), may hold values from 0.25 to 1.75
- ln1_bias: bfloat16 [2, 192], P('section'), may hold values from -3 to 3
- q_weight: bfloat16 [2, 192, 192], P('section'), may hold values from -0.4375 to 0.4375
- q_bias: bfloat16 [2, 192], P('section'), may hold values from -3 to 3
- kv_weight: bfloat16 [192, 384], replicated, may hold values from -0.4375 to 0.4375
- v_bias: bfloat16 [192], replicated, may hold values from -3 to 3
- out_weight: bfloat16 [2, 192, 192], P('section'), may hold values from -1.25 to 1.25
- out_bias: bfloat16 [2, 192], P('section'), may hold values from -3 to 3
- rel_table: bfloat16 [2, 6, 343], P('section'), may hold values from -4 to 4
- ln2_gain: bfloat16 [2, 192], P('section'), may hold values from 0.25 to 1.75
- ln2_bias: bfloat16 [2, 192], P('section'), may hold values from -3 to 3
- up_weight: bfloat16 [2, 192, 768], P('section'), may hold values from -0.4375 to 0.4375
- up_bias: bfloat16 [2, 768], P('section'), may hold values from -3 to 3
- down_weight: bfloat16 [2, 768, 192], P('section'), may hold values from -0.21875 to 0.21875
- down_bias: bfloat16 [2, 192], P('section'), may hold values from -3 to 3
Outputs:
- ends: float32 [2, 3, 128, 16, 32, 192], P('section', None, 'tok')
- ln1_gain_grad: float32 [2, 192], P('section')
- ln1_bias_grad: float32 [2, 192], P('section')
- q_weight_grad: float32 [2, 192, 192], P('section')
- q_bias_grad: float32 [2, 192], P('section')
- kv_weight_grad: float32 [2, 192, 384], P('section')
- v_bias_grad: float32 [2, 192], P('section')
- out_weight_grad: float32 [2, 192, 192], P('section')
- out_bias_grad: float32 [2, 192], P('section')
- rel_table_grad: float32 [2, 6, 343], P('section')
- ln2_gain_grad: float32 [2, 192], P('section')
- ln2_bias_grad: float32 [2, 192], P('section')
- up_weight_grad: float32 [2, 192, 768], P('section')
- up_bias_grad: float32 [2, 768], P('section')
- down_weight_grad: float32 [2, 768, 192], P('section')
- down_bias_grad: float32 [2, 192], P('section')
All inputs are finite; a program needn't handle non-finite values.
Results may differ from a plain program's by a relative error of at most 0.012.
The roundings to bfloat16 on the way count: a program that leaves them out, or rounds other values in their place, can miss the bound.
Values may be sent and summed in bfloat16 or wider, within the bound.
A program may use at most 512 MiB of HBM per device.

v0:
```python
import jax
import jax.numpy as jnp
from jax import lax
from jax.sharding import PartitionSpec as P

HEADS = 6
HD = 32
WIN = 4
SHIFT = 2


eps_norm = 1e-05
mask_fill = -100.0
root_half = 0.7071067811865476
inv_root_two_pi = 0.3989422804014327


def shifted(value, axis, steps):
    count = lax.axis_size(axis)
    pairs = [(source, (source + steps) % count) for source in range(count)]
    return lax.ppermute(value, axis, pairs)


def shifted_2(array, axis, by):
    count = lax.axis_size(axis)
    pairs = [(i, i + by) for i in range(count) if 0 <= i + by < count]
    return lax.ppermute(array, axis, pairs)


def to_windows(field_rows):
    planes, rows_y, rows_z, channels = field_rows.shape
    blocks = field_rows.reshape(
        planes // WIN, WIN, rows_y // WIN, WIN, rows_z // WIN, WIN, channels
    )
    return blocks.transpose(0, 2, 4, 1, 3, 5, 6).reshape(-1, WIN**3, channels)


def from_windows(windows, planes, rows_y, rows_z):
    channels = windows.shape[-1]
    blocks = windows.reshape(planes // WIN, rows_y // WIN, rows_z // WIN, WIN, WIN, WIN, channels)
    return blocks.transpose(0, 3, 1, 4, 2, 5, 6).reshape(planes, rows_y, rows_z, channels)


def relative_index():
    cell_ids = jnp.arange(WIN**3)
    cell_x = cell_ids // (WIN * WIN)
    cell_y = cell_ids // WIN % WIN
    cell_z = cell_ids % WIN
    span_size = 2 * WIN - 1
    return (
        (
            (cell_x[:, None] - cell_x[None, :] + WIN - 1) * span_size
            + cell_y[:, None]
            - cell_y[None, :]
            + WIN
            - 1
        )
        * span_size
        + cell_z[:, None]
        - cell_z[None, :]
        + WIN
        - 1
    )


def region_ids(coords, length):
    return (coords >= length - WIN).astype(jnp.int32) + (coords >= length - SHIFT).astype(jnp.int32)


def roll_block(stacked, rim_slab):
    joined = jnp.concatenate([stacked[:, SHIFT:], rim_slab], 1)
    return jnp.roll(joined, (-SHIFT, -SHIFT), (2, 3))


def unroll_block(stacked, rim_slab):
    joined = jnp.concatenate([rim_slab, stacked[:, :-SHIFT]], 1)
    return jnp.roll(joined, (SHIFT, SHIFT), (2, 3))


def project(left_side, weight):
    return jnp.dot(left_side, weight, preferred_element_type=jnp.float32)


def input_grad(grad_rows, weight):
    return lax.dot_general(
        grad_rows,
        weight,
        (((grad_rows.ndim - 1,), (1,)), ((), ())),
        preferred_element_type=jnp.float32,
    )


def weight_grad(left_side, grad_rows):
    flat_left = left_side.reshape(-1, left_side.shape[-1])
    flat_grad = grad_rows.reshape(-1, grad_rows.shape[-1])
    return lax.dot_general(
        flat_left, flat_grad, (((0,), (0,)), ((), ())), preferred_element_type=jnp.float32
    )


def row_sum(grad_rows):
    return jnp.sum(grad_rows, (0, 1, 2), dtype=jnp.float32)


def norm_forward(field_rows, gain_vec, offset):
    mean_value = jnp.mean(field_rows, -1, keepdims=True)
    centered = field_rows - mean_value
    inv_std = lax.rsqrt(jnp.mean(centered * centered, -1, keepdims=True) + eps_norm)
    unit_rows = centered * inv_std
    return (unit_rows * gain_vec + offset, unit_rows, inv_std)


def norm_backward(grad_rows, unit_rows, inv_std, gain_vec):
    scaled = grad_rows * gain_vec
    back_rows = inv_std * (
        scaled
        - jnp.mean(scaled, -1, keepdims=True)
        - unit_rows * jnp.mean(scaled * unit_rows, -1, keepdims=True)
    )
    return (back_rows, jnp.sum(grad_rows * unit_rows, (0, 1, 2)), jnp.sum(grad_rows, (0, 1, 2)))


def gelu_slope(pre_act):
    return (
        0.5 * (1.0 + lax.erf(pre_act * root_half))
        + pre_act * jnp.exp(-0.5 * pre_act * pre_act) * inv_root_two_pi
    )


def split_heads(rows):
    return rows.reshape(rows.shape[0], WIN**3, HEADS, HD)


def window_scores(queries, key_rows, bias_add):
    return (
        jnp.einsum(
            "wqhd,wkhd->whqk",
            split_heads(queries),
            split_heads(key_rows),
            preferred_element_type=jnp.float32,
        )
        * HD ** (-0.5)
        + bias_add
    )


def attend(queries, key_rows, value_rows, bias_add):
    scores = window_scores(queries, key_rows, bias_add)
    row_peak = jnp.max(scores, -1, keepdims=True)
    exponent = jnp.exp(scores - row_peak)
    totals = jnp.sum(exponent, -1, keepdims=True)
    soft_probs = (exponent / totals).astype(jnp.bfloat16)
    mixed_rows = jnp.einsum(
        "whqk,wkhd->wqhd", soft_probs, split_heads(value_rows), preferred_element_type=jnp.float32
    )
    return (mixed_rows.reshape(queries.shape[0], WIN**3, -1), row_peak + jnp.log(totals))


def attend_back(queries, key_rows, value_rows, bias_add, log_total, grad_mixed):
    soft_probs = jnp.exp(window_scores(queries, key_rows, bias_add) - log_total)
    heads_g = split_heads(grad_mixed)
    d_probs = jnp.einsum(
        "wqhd,wkhd->whqk", heads_g, split_heads(value_rows), preferred_element_type=jnp.float32
    )
    d_values = jnp.einsum(
        "whqk,wqhd->wkhd",
        soft_probs.astype(jnp.bfloat16),
        heads_g,
        preferred_element_type=jnp.float32,
    )
    d_scores = (soft_probs * (d_probs - jnp.sum(d_probs * soft_probs, -1, keepdims=True))).astype(
        jnp.bfloat16
    )
    d_queries = jnp.einsum(
        "whqk,wkhd->wqhd", d_scores, split_heads(key_rows), preferred_element_type=jnp.float32
    ) * HD ** (-0.5)
    d_keys = jnp.einsum(
        "whqk,wqhd->wkhd", d_scores, split_heads(queries), preferred_element_type=jnp.float32
    ) * HD ** (-0.5)
    windows_count = queries.shape[0]
    return (
        d_queries.reshape(windows_count, WIN**3, -1),
        d_keys.reshape(windows_count, WIN**3, -1),
        d_values.reshape(windows_count, WIN**3, -1),
        jnp.sum(d_scores, 0, dtype=jnp.float32),
    )


def body(
    tokens,
    cotangent,
    ln1_gain,
    ln1_bias,
    q_weight,
    q_bias,
    kv_weight,
    v_bias,
    out_weight,
    out_bias,
    rel_table,
    ln2_gain,
    ln2_bias,
    up_weight,
    up_bias,
    down_weight,
    down_bias,
):
    batches = tokens.shape[0]
    planes, rows_y, rows_z, channels = tokens.shape[1:]
    is_encoder = lax.axis_index("section") == 0
    enc_flag = is_encoder.astype(jnp.float32)
    gain_one = ln1_gain[0].astype(jnp.float32)
    bias_one = ln1_bias[0].astype(jnp.float32)
    gain_two = ln2_gain[0].astype(jnp.float32)
    bias_two = ln2_bias[0].astype(jnp.float32)
    q_mat = q_weight[0]
    q_vec = q_bias[0].astype(jnp.float32)
    out_mat = out_weight[0]
    out_vec = out_bias[0].astype(jnp.float32)
    up_mat = up_weight[0]
    up_vec = up_bias[0].astype(jnp.float32)
    down_mat = down_weight[0]
    down_vec = down_bias[0].astype(jnp.float32)
    value_vec = v_bias.astype(jnp.float32)
    kv_vec = jnp.concatenate([jnp.zeros_like(value_vec), value_vec])
    span_size = 2 * WIN - 1
    one_hot = (relative_index().reshape(-1)[:, None] == jnp.arange(span_size**3)[None, :]).astype(
        jnp.float32
    )
    table_rows = rel_table[0].astype(jnp.float32)
    bias_heads = jnp.dot(one_hot, table_rows.T, precision=lax.Precision.HIGHEST).T.reshape(
        HEADS, WIN**3, WIN**3
    )
    span_x = planes * lax.axis_size("tok")
    coord_x = lax.axis_index("tok") * planes + jnp.arange(planes)
    region_field = (
        region_ids(coord_x, span_x)[:, None, None] * 9
        + region_ids(jnp.arange(rows_y), rows_y)[None, :, None] * 3
        + region_ids(jnp.arange(rows_z), rows_z)[None, None, :]
    )
    win_ids = to_windows(region_field[..., None])[..., 0]
    mask_add = jnp.where(win_ids[:, :, None] == win_ids[:, None, :], 0.0, mask_fill).astype(
        jnp.float32
    ) * (1.0 - enc_flag)
    bias_add = bias_heads[None] + mask_add[:, None]
    stack_count = 3
    handed = jnp.zeros((stack_count, planes, rows_y, rows_z, channels), jnp.bfloat16)
    kept_steps = []
    outputs_y = []
    for step_index in range(batches + 1):
        feed_rows = tokens[min(step_index, batches - 1)].astype(jnp.float32)
        entry_field = jnp.where(is_encoder, feed_rows, handed[0].astype(jnp.float32))
        normed, unit_one, inv_one = norm_forward(entry_field, gain_one, bias_one)
        left_one = normed.astype(jnp.bfloat16)
        queries = (project(left_one, q_mat) + q_vec).astype(jnp.bfloat16)
        both_rows = project(left_one, kv_weight) + kv_vec
        key_rows = jnp.where(is_encoder, both_rows[..., :channels].astype(jnp.bfloat16), handed[1])
        value_rows = jnp.where(
            is_encoder, both_rows[..., channels:].astype(jnp.bfloat16), handed[2]
        )
        win_q = to_windows(queries)
        win_k = to_windows(key_rows)
        win_v = to_windows(value_rows)
        attended, log_total = attend(win_q, win_k, win_v, bias_add)
        attended_low = from_windows(attended, planes, rows_y, rows_z).astype(jnp.bfloat16)
        middle = entry_field + project(attended_low, out_mat) + out_vec
        normed_two, unit_two, inv_two = norm_forward(middle, gain_two, bias_two)
        left_two = normed_two.astype(jnp.bfloat16)
        pre_act = project(left_two, up_mat) + up_vec
        hidden = jax.nn.gelu(pre_act, approximate=False).astype(jnp.bfloat16)
        result = middle + project(hidden, down_mat) + down_vec
        kept_steps.append(
            (
                unit_one,
                inv_one,
                left_one,
                win_q,
                win_k,
                win_v,
                log_total,
                attended_low,
                unit_two,
                inv_two,
                left_two,
                pre_act,
                hidden,
            )
        )
        if step_index >= 1:
            tail_slab = shifted(result[None, -SHIFT:].astype(jnp.bfloat16), "tok", 1).astype(
                jnp.float32
            )
            outputs_y.append(unroll_block(result[None], tail_slab)[0])
        if step_index < batches:
            packed = jnp.stack([result.astype(jnp.bfloat16), key_rows, value_rows])
            moved_stack = shifted_2(packed, "section", 1)
            rim_slab = shifted(moved_stack[:, :SHIFT], "tok", -1)
            handed = roll_block(moved_stack, rim_slab)
    returned = jnp.zeros((3, planes, rows_y, rows_z, channels), jnp.bfloat16)
    small_totals = None
    deferred = []
    d_token_list = [None] * batches
    for back_index in range(batches + 1):
        late_batch = batches - 1 - back_index
        if late_batch >= 0:
            cot_rows = cotangent[late_batch][None]
            cot_slab = shifted(cot_rows[:, :SHIFT], "tok", -1)
            from_output = roll_block(cot_rows, cot_slab)[0].astype(jnp.float32)
        else:
            from_output = jnp.zeros((planes, rows_y, rows_z, channels), jnp.float32)
        (
            unit_one,
            inv_one,
            left_one,
            win_q,
            win_k,
            win_v,
            log_total,
            attended_low,
            unit_two,
            inv_two,
            left_two,
            pre_act,
            hidden,
        ) = kept_steps[batches - back_index]
        d_result = jnp.where(is_encoder, returned[0].astype(jnp.float32), from_output)
        d_down = d_result.astype(jnp.bfloat16)
        d_hidden = input_grad(d_down, down_mat)
        d_pre = (d_hidden * gelu_slope(pre_act)).astype(jnp.bfloat16)
        back_two, d_gain_two, d_bias_two = norm_backward(
            input_grad(d_pre, up_mat), unit_two, inv_two, gain_two
        )
        d_middle = d_result + back_two
        d_branch = d_middle.astype(jnp.bfloat16)
        d_attended = to_windows(input_grad(d_branch, out_mat).astype(jnp.bfloat16))
        d_query_win, d_key_win, d_value_win, d_bias_heads = attend_back(
            win_q, win_k, win_v, bias_add, log_total, d_attended
        )
        d_queries = from_windows(d_query_win, planes, rows_y, rows_z).astype(jnp.bfloat16)
        d_keys = from_windows(d_key_win, planes, rows_y, rows_z) + returned[1].astype(jnp.float32)
        d_values = from_windows(d_value_win, planes, rows_y, rows_z) + returned[2].astype(
            jnp.float32
        )
        d_skip = jnp.concatenate([d_keys, d_values], -1).astype(jnp.bfloat16)
        d_normed_one = input_grad(d_queries, q_mat) + input_grad(d_skip, kv_weight) * enc_flag
        back_one, d_gain_one, d_bias_one = norm_backward(d_normed_one, unit_one, inv_one, gain_one)
        d_entry = d_middle + back_one
        d_table = jnp.dot(d_bias_heads.reshape(HEADS, -1), one_hot, precision=lax.Precision.HIGHEST)
        step_small = (d_gain_one, d_bias_one, d_table, d_gain_two, d_bias_two)
        if small_totals is None:
            small_totals = step_small
        else:
            small_totals = jax.tree.map(jnp.add, small_totals, step_small)
        deferred.append(
            (left_one, d_queries, attended_low, d_branch, left_two, d_pre, hidden, d_down, d_skip)
        )
        if back_index >= 1:
            d_token_list[batches - back_index] = d_entry
        if back_index < batches:
            packed_back = jnp.stack(
                [d_entry.astype(jnp.bfloat16), d_skip[..., :channels], d_skip[..., channels:]]
            )
            back_slab = shifted(packed_back[:, -SHIFT:], "tok", 1)
            returned = shifted_2(unroll_block(packed_back, back_slab), "section", -1)

    def pick_slot(later, earlier):
        return jnp.where(is_encoder, later, earlier)

    heavy_totals = None
    for slot_index in range(batches):
        left_one, d_queries, attended_low, d_branch, left_two, d_pre, hidden, d_down, d_skip = (
            jax.tree.map(pick_slot, deferred[slot_index + 1], deferred[slot_index])
        )
        step_heavy = (
            weight_grad(left_one, d_queries),
            row_sum(d_queries),
            weight_grad(attended_low, d_branch),
            row_sum(d_branch),
            weight_grad(left_two, d_pre),
            row_sum(d_pre),
            weight_grad(hidden, d_down),
            row_sum(d_down),
            weight_grad(left_one, d_skip) * enc_flag,
            row_sum(d_skip[..., channels:]) * enc_flag,
        )
        if heavy_totals is None:
            heavy_totals = step_heavy
        else:
            heavy_totals = jax.tree.map(jnp.add, heavy_totals, step_heavy)
    ends = jnp.where(is_encoder, jnp.stack(d_token_list), jnp.stack(outputs_y))[None]
    t_gain_one, t_bias_one, t_table, t_gain_two, t_bias_two = small_totals
    (
        t_q_mat,
        t_q_vec,
        t_out_mat,
        t_out_vec,
        t_up_mat,
        t_up_vec,
        t_down_mat,
        t_down_vec,
        t_kv_mat,
        t_kv_vec,
    ) = heavy_totals
    summed = lax.psum(
        (
            t_gain_one,
            t_bias_one,
            t_q_mat,
            t_q_vec,
            t_out_mat,
            t_out_vec,
            t_table,
            t_gain_two,
            t_bias_two,
            t_up_mat,
            t_up_vec,
            t_down_mat,
            t_down_vec,
        ),
        "tok",
    )
    kv_total, vb_total = lax.psum((t_kv_mat, t_kv_vec), ("section", "tok"))
    (
        s_gain_one,
        s_bias_one,
        s_q_mat,
        s_q_vec,
        s_out_mat,
        s_out_vec,
        s_table,
        s_gain_two,
        s_bias_two,
        s_up_mat,
        s_up_vec,
        s_down_mat,
        s_down_vec,
    ) = summed
    return (
        ends,
        s_gain_one[None],
        s_bias_one[None],
        s_q_mat[None],
        s_q_vec[None],
        kv_total[None],
        vb_total[None],
        s_out_mat[None],
        s_out_vec[None],
        s_table[None],
        s_gain_two[None],
        s_bias_two[None],
        s_up_mat[None],
        s_up_vec[None],
        s_down_mat[None],
        s_down_vec[None],
    )


def solution(mesh):
    in_specs = (
        P(None, "tok", None, None, None),
        P(None, "tok", None, None, None),
        P("section", None),
        P("section", None),
        P("section", None, None),
        P("section", None),
        P(),
        P(),
        P("section", None, None),
        P("section", None),
        P("section", None, None),
        P("section", None),
        P("section", None),
        P("section", None, None),
        P("section", None),
        P("section", None, None),
        P("section", None),
    )
    out_specs = (
        P("section", None, "tok", None, None, None),
        P("section", None),
        P("section", None),
        P("section", None, None),
        P("section", None),
        P("section", None, None),
        P("section", None),
        P("section", None, None),
        P("section", None),
        P("section", None, None),
        P("section", None),
        P("section", None),
        P("section", None, None),
        P("section", None),
        P("section", None, None),
        P("section", None),
    )
    return jax.shard_map(body, mesh=mesh, in_specs=in_specs, out_specs=out_specs, check_vma=False)
```

profile of v0, /device:TPU:0, one launch (start us, length us, event | category | flops | bytes accessed | tf_op | source)
XLA Modules:
  0.0 2572.8 jit_solution(13918760622706101460)
XLA Ops:
  55.3 10.5 copy.416
  72.1 10.5 copy.412
  118.7 13.5 copy.418
  158.9 29.3 %fusion.2 = bf16[8,16,32,768]{3,2,1,0:T(8,128)(2,1)S(1)} fusion(f32[8,16,32,768]{3,2,1,0:T(8,128)S(1)} %get-tuple-element.221, f32[768]{0:T(1024)S(1)} %convert_reduce_fusion.19, u16[8,32,768]{2,1,0:T(8,128)(2,1)S(1)} %get-tuple-element.109, u16[8,32,768]{2,1,0:T(8,128)(2,1)S(1)} %get-tuple-element.108), kind=kLoop, calls=%fused_computation.14 | loop fusion | flops 223346688 | bytes 19663872 | tf_op jit(solution)/shard_map/convert_element_type | solution.py:270
  213.3 33.7 %collective-permute-done.2 = bf16[3,2,16,32,192]{4,3,2,1,0:T(8,128)(2,1)S(1)} collective-permute-done((bf16[3,2,16,32,192]{4,3,2,1,0:T(8,128)(2,1)S(1)}, bf16[3,2,16,32,192]{4,3,2,1,0:T(8,128)(2,1)S(1)}, u32[]{:S(2)}, u32[]{:S(2)}) %collective-permute-start.2) | collective-permute-done | bytes 1179680 | tf_op jit(solution)/shard_map/ppermute | solution.py:21
  301.8 10.9 copy.425
  319.1 10.5 copy.424
  363.7 13.5 copy.427
  410.9 28.8 %fusion.5 = bf16[8,16,32,768]{3,2,1,0:T(8,128)(2,1)S(1)} fusion(f32[8,16,32,768]{3,2,1,0:T(8,128)S(1)} %get-tuple-element.226, f32[768]{0:T(1024)S(1)} %convert_reduce_fusion.19, u16[8,32,768]{2,1,0:T(8,128)(2,1)S(1)} %get-tuple-element.107, u16[8,32,768]{2,1,0:T(8,128)(2,1)S(1)} %get-tuple-element.106), kind=kLoop, calls=%fused_computation.17 | loop fusion | flops 223346688 | bytes 19663872 | tf_op jit(solution)/shard_map/convert_element_type | solution.py:270
  464.7 33.7 %collective-permute-done.4 = bf16[3,2,16,32,192]{4,3,2,1,0:T(8,128)(2,1)S(1)} collective-permute-done((bf16[3,2,16,32,192]{4,3,2,1,0:T(8,128)(2,1)S(1)}, bf16[3,2,16,32,192]{4,3,2,1,0:T(8,128)(2,1)S(1)}, u32[]{:S(2)}, u32[]{:S(2)}) %collective-permute-start.4) | collective-permute-done | bytes 1179680 | tf_op jit(solution)/shard_map/ppermute | solution.py:21
  553.6 10.6 copy.434
  570.5 10.5 copy.433
  615.3 13.5 copy.436
  663.0 29.2 %fusion.8 = bf16[8,16,32,768]{3,2,1,0:T(8,128)(2,1)S(1)} fusion(f32[8,16,32,768]{3,2,1,0:T(8,128)S(1)} %get-tuple-element.233, f32[768]{0:T(1024)S(1)} %convert_reduce_fusion.19, u16[8,32,768]{2,1,0:T(8,128)(2,1)S(1)} %get-tuple-element.105, u16[8,32,768]{2,1,0:T(8,128)(2,1)S(1)} %get-tuple-element.104), kind=kLoop, calls=%fused_computation.20 | loop fusion | flops 223346688 | bytes 19663872 | tf_op jit(solution)/shard_map/convert_element_type | solution.py:270
  720.1 42.1 %collective-permute-done = bf16[1,2,16,32,192]{4,3,2,1,0:T(8,128)(2,1)S(1)} collective-permute-done((bf16[1,2,16,32,192]{4,3,2,1,0:T(8,128)(2,1)S(1)}, bf16[1,2,16,32,192]{4,3,2,1,0:T(8,128)(2,1)S(1)}, u32[]{:S(2)}, u32[]{:S(2)}) %collective-permute-start) | collective-permute-done | bytes 393248 | tf_op jit(solution)/shard_map/ppermute | solution.py:21
  884.1 14.6 broadcast_select_fusion.5
  898.7 12.8 copy.445
  992.2 13.6 copy.460
  1005.8 10.6 reshape_reshape.116
  1030.8 14.2 multiply_reduce_fusion.3
  1044.9 10.9 convert_reduce_fusion.6
  1062.4 12.9 copy.456
  1095.0 13.5 copy.452
  1141.2 39.3 %collective-permute-done.7 = bf16[3,2,16,32,192]{4,3,2,1,0:T(8,128)(2,1)S(1)} collective-permute-done((bf16[3,2,16,32,192]{4,3,2,1,0:T(8,128)(2,1)S(1)}, bf16[3,2,16,32,192]{4,3,2,1,0:T(8,128)(2,1)S(1)}, u32[]{:S(2)}, u32[]{:S(2)}) %collective-permute-start.7) | collective-permute-done | bytes 1179680 | tf_op jit(solution)/shard_map/ppermute | solution.py:21
  1180.5 10.9 fusion.83
  1205.2 10.9 collective-permute-done.9
  1267.1 10.6 fusion.168
  1277.8 13.9 multiply_reduce_fusion.2
  1291.7 11.1 convert_reduce_fusion.5
  1309.9 12.9 copy.469
  1344.7 15.1 copy.473
  1359.8 11.8 reshape_reshape.118
  1383.9 15.3 copy.477
  1399.2 11.8 reshape_reshape.119
  1444.4 39.1 %collective-permute-done.10 = bf16[3,2,16,32,192]{4,3,2,1,0:T(8,128)(2,1)S(1)} collective-permute-done((bf16[3,2,16,32,192]{4,3,2,1,0:T(8,128)(2,1)S(1)}, bf16[3,2,16,32,192]{4,3,2,1,0:T(8,128)(2,1)S(1)}, u32[]{:S(2)}, u32[]{:S(2)}) %collective-permute-start.10) | collective-permute-done | bytes 1179680 | tf_op jit(solution)/shard_map/ppermute | solution.py:21
  1483.6 10.9 fusion.80
  1551.1 10.7 fusion.171
  1561.8 14.0 multiply_reduce_fusion.1
  1575.7 11.1 convert_reduce_fusion.4
  1594.0 13.1 copy.484
  1629.0 15.1 copy.488
  1644.1 11.8 reshape_reshape.121
  1668.2 15.3 copy.492
  1683.5 11.9 reshape_reshape.122
  1731.4 48.7 %collective-permute-done.15 = bf16[1,2,16,32,192]{4,3,2,1,0:T(8,128)(2,1)S(1)} collective-permute-done((bf16[1,2,16,32,192]{4,3,2,1,0:T(8,128)(2,1)S(1)}, bf16[1,2,16,32,192]{4,3,2,1,0:T(8,128)(2,1)S(1)}, u32[]{:S(2)}, u32[]{:S(2)}) %collective-permute-start.15) | collective-permute-done | bytes 393248 | tf_op jit(solution)/shard_map/ppermute | solution.py:21
  1782.2 11.0 fusion.77
  1794.6 28.9 %fusion.35 = bf16[8,16,32,768]{3,2,1,0:T(8,128)(2,1)S(1)} fusion(f32[8,16,32,768]{3,2,1,0:T(8,128)S(1)} %bitcast.892, f32[768]{0:T(1024)S(1)} %convert_reduce_fusion.19, u16[8,32,768]{2,1,0:T(8,128)(2,1)S(1)} %copy-done.192, u16[8,32,768]{2,1,0:T(8,128)(2,1)S(1)} %copy-done.191), kind=kLoop, calls=%fused_computation.47 | loop fusion | flops 223346688 | bytes 19663872 | tf_op jit(solution)/shard_map/convert_element_type | solution.py:270
  1835.8 12.7 copy.512
  1866.2 12.7 copy.514
  1897.1 12.7 copy.516
  1956.0 14.1 convert_reduce_fusion.1
  2012.1 10.7 fusion.174
  2022.8 14.0 multiply_reduce_fusion
  2036.7 11.1 convert_reduce_fusion.3
  2056.0 15.1 copy.503
  2071.2 12.0 reshape_reshape.124
  2095.4 15.1 copy.507
  2110.6 11.8 reshape_reshape.125
  2134.7 13.3 convert_reduce_fusion.8
  2148.1 10.5 broadcast_select_fusion.8
  2175.1 13.2 copy.499
  2254.6 40.7 %psum.110 = f32[1,192]{1,0:T(1,128)} all-reduce(f32[1,192]{1,0:T(1,128)S(1)} %bitcast.934), channel_id=1, replica_groups=mesh['section'=2,'tok'=16] {'section','tok'}, use_global_device_ids=true, to_apply=%region_63.64 | all-reduce | flops 192 | bytes 1536 | tf_op jit(solution)/shard_map/psum | solution.py:422
  2304.5 76.7 %all-reduce.1 = (f32[1,192]{1,0:T(1,128)}, f32[1,192]{1,0:T(1,128)}, f32[1,192]{1,0:T(1,128)}, f32[1,192]{1,0:T(1,128)}, f32[1,6,343]{2,1,0:T(8,128)S(1)}, /*ind...) all-reduce(f32[1,192]{1,0:T(1,128)S(1)} %bitcast.930, ...), channel_id=1, replica_groups=mesh['section'=2,'tok'=16] {'tok'}, use_global_device_ids=true, to_apply=%region_48.49 | all-reduce | flops 4170 | bytes 33360 | tf_op jit(solution)/shard_map/psum | solution.py:404
  2431.1 126.0 %all-reduce.8.cloned.1.call-done = (f32[1,192,192]{2,1,0:T(8,128)}, f32[1,192,192]{2,1,0:T(8,128)}, f32[1,192,768]{2,1,0:T(8,128)}, f32[1,768,192]{1,2,0:T(8,128)}) async-done(((f32[1,192,192]{2,1,0:T(8,128)}, f32[1,192,192]{2,1,0:T(8,128)}, f32[1,192,768]{2,1,0:T(8,128)}, f32[1,768,192]{1,2,0:T(8,128)}), (f32[1,192,192]{2,1,0:T(8,128)}, f32[1,192,192]{2,1,0:T(8,128)}, f32[1,192,768]{2,1,0:T(8,128)}, ...) | async-done | bytes 1474576 | tf_op jit(solution)/shard_map/psum | solution.py:404
  (968 shorter events, 1323.0 us)
Async XLA Ops:
  7.2 145.5 %copy-start = (bf16[1,192,768]{2,1,0:T(8,128)(2,1)S(1)}, bf16[1,192,768]{2,1,0:T(8,128)(2,1)}, u32[]{:S(2)}) copy-start(bf16[1,192,768]{2,1,0:T(8,128)(2,1)} %param.30) | copy-start | bytes 884740
  7.2 14.2 copy-start.232
  7.2 2423.9 %all-reduce.6.cloned.1.call-start = ((), (), s32[]{:S(2)}) async-start(), calls=%async_computation | async-start | bytes 589824 | tf_op jit(solution)/shard_map/psum | solution.py:422
  18.8 13.4 copy-start.187
  151.3 36.9 %copy-start.68 = (f32[8,16,32,192]{3,2,1,0:T(8,128)}, f32[8,16,32,192]{3,2,1,0:T(8,128)S(1)}, u32[]{:S(2)}) copy-start(f32[8,16,32,192]{3,2,1,0:T(8,128)S(1)} %get-tuple-element.220) | copy-start | bytes 9437188
  158.8 29.3 %copy-start.82 = (f32[8,16,32,768]{3,2,1,0:T(8,128)}, f32[8,16,32,768]{3,2,1,0:T(8,128)S(1)}, u32[]{:S(2)}) copy-start(f32[8,16,32,768]{3,2,1,0:T(8,128)S(1)} %get-tuple-element.221) | copy-start | bytes 37748740
  158.9 29.3 %copy-start.120 = (bf16[1,768,192]{1,2,0:T(8,128)(2,1)S(1)}, bf16[1,768,192]{1,2,0:T(8,128)(2,1)}, u32[]{:S(2)}) copy-start(bf16[1,768,192]{1,2,0:T(8,128)(2,1)} %param.32) | copy-start | bytes 884740
  194.1 12.1 collective-permute-start.1
  206.4 40.5 %collective-permute-start.2 = (bf16[3,2,16,32,192]{4,3,2,1,0:T(8,128)(2,1)S(1)}, bf16[3,2,16,32,192]{4,3,2,1,0:T(8,128)(2,1)S(1)}, u32[]{:S(2)}, u32[]{:S(2)}) collective-permute-start(bf16[3,2,16,32,192]{4,3,2,1,0:T(8,128)(2,1)S(1)} %slice.477), channel_id=1, source_target_pairs={{0,15},{1,0},{2,1},{3,2},{4,3},{5,4},{6,5},{7,6},{8,7},{9,8},{10,9... | collective-permute-start | bytes 3538952 | tf_op jit(solution)/shard_map/ppermute | solution.py:21
  397.0 42.7 %copy-start.7 = (f32[8,16,32,192]{3,2,1,0:T(8,128)}, f32[8,16,32,192]{3,2,1,0:T(8,128)S(1)}, u32[]{:S(2)}) copy-start(f32[8,16,32,192]{3,2,1,0:T(8,128)S(1)} %get-tuple-element.225) | copy-start | bytes 9437188
  410.9 28.8 %copy-start.121 = (bf16[1,768,192]{1,2,0:T(8,128)(2,1)S(1)}, bf16[1,768,192]{1,2,0:T(8,128)(2,1)}, u32[]{:S(2)}) copy-start(bf16[1,768,192]{1,2,0:T(8,128)(2,1)} %param.32) | copy-start | bytes 884740
  446.6 11.2 collective-permute-start.3
  458.0 40.3 %collective-permute-start.4 = (bf16[3,2,16,32,192]{4,3,2,1,0:T(8,128)(2,1)S(1)}, bf16[3,2,16,32,192]{4,3,2,1,0:T(8,128)(2,1)S(1)}, u32[]{:S(2)}, u32[]{:S(2)}) collective-permute-start(bf16[3,2,16,32,192]{4,3,2,1,0:T(8,128)(2,1)S(1)} %slice.487), channel_id=1, source_target_pairs={{0,15},{1,0},{2,1},{3,2},{4,3},{5,4},{6,5},{7,6},{8,7},{9,8},{10,9... | collective-permute-start | bytes 3538952 | tf_op jit(solution)/shard_map/ppermute | solution.py:21
  648.7 43.5 %copy-start.5 = (f32[8,16,32,192]{3,2,1,0:T(8,128)}, f32[8,16,32,192]{3,2,1,0:T(8,128)S(1)}, u32[]{:S(2)}) copy-start(f32[8,16,32,192]{3,2,1,0:T(8,128)S(1)} %get-tuple-element.232) | copy-start | bytes 9437188
  663.0 29.2 %copy-start.122 = (bf16[1,768,192]{1,2,0:T(8,128)(2,1)S(1)}, bf16[1,768,192]{1,2,0:T(8,128)(2,1)}, u32[]{:S(2)}) copy-start(bf16[1,768,192]{1,2,0:T(8,128)(2,1)} %param.32) | copy-start | bytes 884740
  697.2 19.6 slice-start.32
  697.6 19.2 slice-start.33
  699.1 11.4 collective-permute-start.5
  710.6 56.9 %collective-permute-start.6 = (bf16[3,2,16,32,192]{4,3,2,1,0:T(8,128)(2,1)S(1)}, bf16[3,2,16,32,192]{4,3,2,1,0:T(8,128)(2,1)S(1)}, u32[]{:S(2)}, u32[]{:S(2)}) collective-permute-start(bf16[3,2,16,32,192]{4,3,2,1,0:T(8,128)(2,1)S(1)} %slice.497), channel_id=1, source_target_pairs={{0,15},{1,0},{2,1},{3,2},{4,3},{5,4},{6,5},{7,6},{8,7},{9,8},{10,9... | collective-permute-start | bytes 3538952 | tf_op jit(solution)/shard_map/ppermute | solution.py:21
  717.9 44.3 %collective-permute-start = (bf16[1,2,16,32,192]{4,3,2,1,0:T(8,128)(2,1)S(1)}, bf16[1,2,16,32,192]{4,3,2,1,0:T(8,128)(2,1)S(1)}, u32[]{:S(2)}, u32[]{:S(2)}) collective-permute-start(bf16[1,2,16,32,192]{4,3,2,1,0:T(8,128)(2,1)S(1)} %get-tuple-element.197), channel_id=1, source_target_pairs={{0,15},{1,0},{2,1},{3,2},{4,3},{5,4},{6,5},{7,6},{8,7},{9,8},{10,9... | collective-permute-start | bytes 1179656 | tf_op jit(solution)/shard_map/ppermute | solution.py:21
  931.2 25.3 copy-start.14
  931.3 25.3 copy-start.181
  932.6 23.9 copy-start.201
  1141.1 51.7 %copy-start.190 = (bf16[1,2,16,32,192]{4,3,2,1,0:T(8,128)(2,1)S(1)}, bf16[1,2,16,32,192]{4,3,2,1,0:T(8,128)(2,1)}, u32[]{:S(2)}) copy-start(bf16[1,2,16,32,192]{4,3,2,1,0:T(8,128)(2,1)} %get-tuple-element.195) | copy-start | bytes 1179652
  1141.1 53.5 %copy-start.189 = (bf16[1,2,16,32,192]{4,3,2,1,0:T(8,128)(2,1)S(1)}, bf16[1,2,16,32,192]{4,3,2,1,0:T(8,128)(2,1)}, u32[]{:S(2)}) copy-start(bf16[1,2,16,32,192]{4,3,2,1,0:T(8,128)(2,1)} %get-tuple-element.196) | copy-start | bytes 1179652
  1141.2 63.7 %copy-start.36 = (bf16[1,6,16,32,192]{4,3,2,1,0:T(8,128)(2,1)S(1)}, bf16[1,6,16,32,192]{4,3,2,1,0:T(8,128)(2,1)}, u32[]{:S(2)}) copy-start(bf16[1,6,16,32,192]{4,3,2,1,0:T(8,128)(2,1)} %get-tuple-element.198) | copy-start | bytes 3538948
  1141.2 39.4 %collective-permute-start.7 = (bf16[3,2,16,32,192]{4,3,2,1,0:T(8,128)(2,1)S(1)}, bf16[3,2,16,32,192]{4,3,2,1,0:T(8,128)(2,1)S(1)}, u32[]{:S(2)}, u32[]{:S(2)}) collective-permute-start(bf16[3,2,16,32,192]{4,3,2,1,0:T(8,128)(2,1)S(1)} %pad_maximum_fusion.74), channel_id=1, source_target_pairs={{0,1},{1,2},{2,3},{3,4},{4,5},{5,6},{6,7},{7,8},{8,9},{9,10},{10,1... | collective-permute-start | bytes 3538952 | tf_op jit(solution)/shard_map/ppermute | solution.py:21
  1191.4 24.7 copy-start.38
  1191.4 30.0 %collective-permute-start.8 = (bf16[3,8,16,32,192]{4,3,2,1,0:T(8,128)(2,1)}, bf16[3,8,16,32,192]{4,3,2,1,0:T(8,128)(2,1)}, u32[]{:S(2)}, u32[]{:S(2)}) collective-permute-start(bf16[3,8,16,32,192]{4,3,2,1,0:T(8,128)(2,1)} %fusion.83), channel_id=1, source_target_pairs={{16,0},{17,1},{18,2},{19,3},{20,4},{21,5},{22,6},{23,7},{24,8},{25... | collective-permute-start | bytes 14155784 | tf_op jit(solution)/shard_map/ppermute | solution.py:27
  1192.9 12.0 collective-permute-start.12
  1194.7 21.5 collective-permute-start.9
  1220.7 17.8 copy-start.50
  1429.8 53.7 %copy-start.19 = (bf16[8,16,32,192]{3,2,1,0:T(8,128)(2,1)}, bf16[8,16,32,192]{3,2,1,0:T(8,128)(2,1)S(1)}, u32[]{:S(2)}) copy-start(bf16[8,16,32,192]{3,2,1,0:T(8,128)(2,1)S(1)} %get-tuple-element.201) | copy-start | bytes 4718596
  1429.9 53.7 %copy-start.21 = (bf16[8,16,32,192]{3,2,1,0:T(8,128)(2,1)}, bf16[8,16,32,192]{3,2,1,0:T(8,128)(2,1)S(1)}, u32[]{:S(2)}) copy-start(bf16[8,16,32,192]{3,2,1,0:T(8,128)(2,1)S(1)} %get-tuple-element.202) | copy-start | bytes 4718596
  1444.0 63.6 %slice-start.23 = ((s8[12582912]{0:T(1024)(128)(4,1)}), s8[4194304]{0:T(1024)(128)(4,1)S(1)}, s32[]{:S(2)}) async-start(s8[12582912]{0:T(1024)(128)(4,1)} %bitcast.889), calls=%async_computation.25 | async-start | bytes 8388608
  1444.4 52.1 %copy-start.105 = (bf16[1,8,16,32,192]{4,3,2,1,0:T(8,128)(2,1)S(1)}, bf16[1,8,16,32,192]{4,3,2,1,0:T(8,128)(2,1)}, u32[]{:S(2)}) copy-start(bf16[1,8,16,32,192]{4,3,2,1,0:T(8,128)(2,1)} %get-tuple-element.261) | copy-start | bytes 4718596
  1444.4 63.2 %slice-start.24 = ((s8[12582912]{0:T(1024)(128)(4,1)}), s8[4194304]{0:T(1024)(128)(4,1)S(1)}, s32[]{:S(2)}) async-start(s8[12582912]{0:T(1024)(128)(4,1)} %bitcast.889), calls=%async_computation.26 | async-start | bytes 8388608
  1444.4 39.2 %collective-permute-start.10 = (bf16[3,2,16,32,192]{4,3,2,1,0:T(8,128)(2,1)S(1)}, bf16[3,2,16,32,192]{4,3,2,1,0:T(8,128)(2,1)S(1)}, u32[]{:S(2)}, u32[]{:S(2)}) collective-permute-start(bf16[3,2,16,32,192]{4,3,2,1,0:T(8,128)(2,1)S(1)} %pad_maximum_fusion.73), channel_id=1, source_target_pairs={{0,1},{1,2},{2,3},{3,4},{4,5},{5,6},{6,7},{7,8},{8,9},{9,10},{10,1... | collective-permute-start | bytes 3538952 | tf_op jit(solution)/shard_map/ppermute | solution.py:21
  1494.5 13.1 collective-permute-start.11
  1498.8 24.3 copy-start.67
  1499.6 16.6 copy-start.8
  1499.6 16.6 copy-start.164
  1499.6 16.6 copy-start.184
  1714.3 67.9 %copy-start.23 = (bf16[8,16,32,192]{3,2,1,0:T(8,128)(2,1)}, bf16[8,16,32,192]{3,2,1,0:T(8,128)(2,1)S(1)}, u32[]{:S(2)}) copy-start(bf16[8,16,32,192]{3,2,1,0:T(8,128)(2,1)S(1)} %get-tuple-element.193) | copy-start | bytes 4718596
  1714.3 67.9 %copy-start.25 = (bf16[8,16,32,192]{3,2,1,0:T(8,128)(2,1)}, bf16[8,16,32,192]{3,2,1,0:T(8,128)(2,1)S(1)}, u32[]{:S(2)}) copy-start(bf16[8,16,32,192]{3,2,1,0:T(8,128)(2,1)S(1)} %get-tuple-element.194) | copy-start | bytes 4718596
  1728.8 53.3 %collective-permute-start.13 = (bf16[3,2,16,32,192]{4,3,2,1,0:T(8,128)(2,1)S(1)}, bf16[3,2,16,32,192]{4,3,2,1,0:T(8,128)(2,1)S(1)}, u32[]{:S(2)}, u32[]{:S(2)}) collective-permute-start(bf16[3,2,16,32,192]{4,3,2,1,0:T(8,128)(2,1)S(1)} %pad_maximum_fusion.72), channel_id=1, source_target_pairs={{0,1},{1,2},{2,3},{3,4},{4,5},{5,6},{6,7},{7,8},{8,9},{9,10},{10,1... | collective-permute-start | bytes 3538952 | tf_op jit(solution)/shard_map/ppermute | solution.py:21
  1730.2 49.9 %collective-permute-start.15 = (bf16[1,2,16,32,192]{4,3,2,1,0:T(8,128)(2,1)S(1)}, bf16[1,2,16,32,192]{4,3,2,1,0:T(8,128)(2,1)S(1)}, u32[]{:S(2)}, u32[]{:S(2)}) collective-permute-start(bf16[1,2,16,32,192]{4,3,2,1,0:T(8,128)(2,1)S(1)} %slice_bitcast_fusion.13), channel_id=1, source_target_pairs={{0,1},{1,2},{2,3},{3,4},{4,5},{5,6},{6,7},{7,8},{8,9},{9,10},{10,1... | collective-permute-start | bytes 1179656 | tf_op jit(solution)/shard_map/ppermute | solution.py:21
  1731.0 63.4 %slice-start.26 = ((s8[12582912]{0:T(1024)(128)(4,1)}), s8[4194304]{0:T(1024)(128)(4,1)S(1)}, s32[]{:S(2)}) async-start(s8[12582912]{0:T(1024)(128)(4,1)} %bitcast.891), calls=%async_computation.28 | async-start | bytes 8388608
  1731.4 63.1 %slice-start.27 = ((s8[12582912]{0:T(1024)(128)(4,1)}), s8[4194304]{0:T(1024)(128)(4,1)S(1)}, s32[]{:S(2)}) async-start(s8[12582912]{0:T(1024)(128)(4,1)} %bitcast.891), calls=%async_computation.29 | async-start | bytes 8388608
  1782.1 49.5 %collective-permute-start.16 = (bf16[1,2,16,32,192]{4,3,2,1,0:T(8,128)(2,1)}, bf16[1,2,16,32,192]{4,3,2,1,0:T(8,128)(2,1)}, u32[]{:S(2)}, u32[]{:S(2)}) collective-permute-start(bf16[1,2,16,32,192]{4,3,2,1,0:T(8,128)(2,1)} %slice_bitcast_fusion.12), channel_id=1, source_target_pairs={{0,1},{1,2},{2,3},{3,4},{4,5},{5,6},{6,7},{7,8},{8,9},{9,10},{10,1... | collective-permute-start | bytes 1179656 | tf_op jit(solution)/shard_map/ppermute | solution.py:21
  1793.2 162.0 %collective-permute-start.14 = (bf16[3,8,16,32,192]{4,3,2,1,0:T(8,128)(2,1)}, bf16[3,8,16,32,192]{4,3,2,1,0:T(8,128)(2,1)}, u32[]{:S(2)}, u32[]{:S(2)}) collective-permute-start(bf16[3,8,16,32,192]{4,3,2,1,0:T(8,128)(2,1)} %fusion.77), channel_id=1, source_target_pairs={{16,0},{17,1},{18,2},{19,3},{20,4},{21,5},{22,6},{23,7},{24,8},{25... | collective-permute-start | bytes 14155784 | tf_op jit(solution)/shard_map/ppermute | solution.py:27
  1794.5 28.9 %copy-start.15 = (f32[8,16,32,192]{3,2,1,0:T(8,128)S(1)}, f32[8,16,32,192]{3,2,1,0:T(8,128)}, u32[]{:S(2)}) copy-start(f32[8,16,32,192]{3,2,1,0:T(8,128)} %copy-done.14) | copy-start | bytes 9437188
  1794.5 28.9 %copy-start.126 = (bf16[1,768,192]{1,2,0:T(8,128)(2,1)S(1)}, bf16[1,768,192]{1,2,0:T(8,128)(2,1)}, u32[]{:S(2)}) copy-start(bf16[1,768,192]{1,2,0:T(8,128)(2,1)} %param.32) | copy-start | bytes 884740
  1827.0 105.9 %collective-permute-start.17 = (bf16[1,2,16,32,192]{4,3,2,1,0:T(8,128)(2,1)}, bf16[1,2,16,32,192]{4,3,2,1,0:T(8,128)(2,1)}, u32[]{:S(2)}, u32[]{:S(2)}) collective-permute-start(bf16[1,2,16,32,192]{4,3,2,1,0:T(8,128)(2,1)} %fusion.333), channel_id=1, source_target_pairs={{0,1},{1,2},{2,3},{3,4},{4,5},{5,6},{6,7},{7,8},{8,9},{9,10},{10,1... | collective-permute-start | bytes 1179656 | tf_op jit(solution)/shard_map/ppermute | solution.py:21
  1955.2 14.9 copy-start.69
  1955.2 14.9 copy-start.177
  1955.2 14.9 copy-start.197
  2134.7 13.3 copy-start.22
  2247.9 47.4 %copy-start.180 = (f32[8,16,32]{2,1,0:T(8,128)S(1)}, f32[8,16,32]{2,1,0:T(8,128)}, u32[]{:S(2)}) copy-start(f32[8,16,32]{2,1,0:T(8,128)} %copy-done.178) | copy-start | bytes 49156
  2247.9 47.4 %copy-start.200 = (f32[8,16,32]{2,1,0:T(8,128)S(1)}, f32[8,16,32]{2,1,0:T(8,128)}, u32[]{:S(2)}) copy-start(f32[8,16,32]{2,1,0:T(8,128)} %copy-done.198) | copy-start | bytes 49156
  2295.6 86.3 %copy-start.182 = (f32[8,16,32]{2,1,0:T(8,128)S(1)}, f32[8,16,32]{2,1,0:T(8,128)}, u32[]{:S(2)}) copy-start(f32[8,16,32]{2,1,0:T(8,128)} %copy-done.181) | copy-start | bytes 49156
  2295.6 86.3 %copy-start.202 = (f32[8,16,32]{2,1,0:T(8,128)S(1)}, f32[8,16,32]{2,1,0:T(8,128)}, u32[]{:S(2)}) copy-start(f32[8,16,32]{2,1,0:T(8,128)} %copy-done.201) | copy-start | bytes 49156
  2295.6 95.5 %slice-start.14 = ((s8[6291456]{0:T(1024)(128)(4,1)}), s8[2097152]{0:T(1024)(128)(4,1)S(1)}, s32[]{:S(2)}) async-start(s8[6291456]{0:T(1024)(128)(4,1)} %bitcast.850), calls=%async_computation.16 | async-start | bytes 4194304
  2302.0 255.0 %all-reduce.8.cloned.1.call-start = ((), (), s32[]{:S(2)}) async-start(), calls=%async_computation.1 | async-start | bytes 3145728 | tf_op jit(solution)/shard_map/psum | solution.py:404
  (233 other events, 1468.1 us)
Sparse Core Ops, SparseCore 0:
  2302.1 127.5 all-reduce.5
  2437.7 119.2 all-reduce.7
where the time goes:
time: 2590 us; the launch traced here: 2570 us
  local copies, waits for them, and re-layouts  1120 us (43%)
  matrix products  452 us (17%)
  waiting for transfers between devices  420 us (16%)
  other arithmetic  410 us (16%)
  blocking collectives  117 us (5%)
  starting transfers between devices  32.1 us (1%)
    another operation x32, local copies, waits for them, and re-layouts, split_heads(): return rows.reshape(rows.shape[0], WIN ** 3, HEADS, HD)  271 us
    ppermute x12, waiting for transfers between devices, shifted(): return lax.ppermute(value, axis, pairs)  258 us
    psum x1, waiting for transfers between devices, body(): lax.psum((t_gain_one, t_bias_one, t_q_mat, t_q_vec, t_out_mat, t_out_vec,...  126 us
    convert_element_type x16, local copies, waits for them, and re-layouts, body(): from_windows(d_query_win, planes, rows_y, rows_z).astype(jnp.bfloat16)  123 us
    convert_element_type x16, local copies, waits for them, and re-layouts, body(): from_windows(attended, planes, rows_y, rows_z).astype(jnp.bfloat16)  119 us
    select_n x18, local copies, waits for them, and re-layouts, pick_slot(): return jnp.where(is_encoder, later, earlier)  117 us
    convert_element_type x4, other arithmetic, body(): hidden = jax.nn.gelu(pre_act, approximate=False).astype(jnp.bfloat16)  116 us
    dot_general x20, matrix products, input_grad(): lax.dot_general(grad_rows, weight, (((grad_rows.ndim - 1,), (1,)), ((), (...  107 us
  transfers between devices with their start and end apart: 20, of which 13 were waited for; matrix products, arithmetic and copies ran while one was open for 9% of the time, Pallas kernels for 0%

commit v1 on v0

v1 whole, which is shorter than its diff:
```python
import functools

import jax
import jax.numpy as jnp
import numpy as np
from jax import lax
from jax.experimental import pallas as pl
from jax.experimental.pallas import tpu as pltpu
from jax.sharding import PartitionSpec as P

HEADS = 6
HD = 32
WIN = 4
SHIFT = 2
CELLS = WIN**3
SPAN = 2 * WIN - 1
HEADS_A = 4
LANES_A = HEADS_A * HD
COLS_A = HEADS_A * CELLS

eps_norm = 1e-05
mask_fill = -100.0
log2_e = 1.4426950408889634
root_half = 0.7071067811865476
inv_root_two_pi = 0.3989422804014327
scale = HD ** (-0.5)
VMEM_BYTES = 56 * 1024 * 1024

F32 = jnp.float32
BF16 = jnp.bfloat16


def nn(left, right):
    return lax.dot_general(left, right, (((1,), (0,)), ((), ())), preferred_element_type=F32)


def nt(left, right):
    return lax.dot_general(left, right, (((1,), (1,)), ((), ())), preferred_element_type=F32)


def tn(left, right):
    return lax.dot_general(left, right, (((0,), (0,)), ((), ())), preferred_element_type=F32)


def order_matrix(rows_z, rolled):
    count = 4 * rows_z
    matrix = np.zeros((count, count), np.float32)
    units = rows_z // 2
    for unit in range(units):
        for dx in range(2):
            for dy in range(2):
                for dz in range(2):
                    z = (2 * (unit + rolled) + dz) % rows_z
                    matrix[unit * 8 + dx * 4 + dy * 2 + dz, (dx * 2 + dy) * rows_z + z] = 1.0
    return matrix


def cell_coords():
    ids = np.arange(CELLS)
    x = 2 * (ids // 32) + ids // 4 % 2
    y = 2 * (ids // 16 % 2) + ids // 2 % 2
    z = 2 * (ids // 8 % 2) + ids % 2
    return x, y, z


def relative_index():
    x, y, z = cell_coords()

    def offset(c):
        return c[None, :] - c[:, None] + WIN - 1

    return (offset(x) * SPAN + offset(y)) * SPAN + offset(z)


def windows_of(pieces):
    count, rows, channels = pieces.shape
    return pieces.reshape(count, rows // 16, 16, channels).transpose(1, 0, 2, 3).reshape(-1, channels)


def pieces_of(windows):
    rows, channels = windows.shape
    return (
        windows.reshape(rows // CELLS, 4, 16, channels)
        .transpose(1, 0, 2, 3)
        .reshape(4, rows // 4, channels)
    )


def roll_rows(pieces, steps):
    return jnp.concatenate([pieces[:, steps:], pieces[:, :steps]], 1)


def normalize(rows):
    mean = jnp.mean(rows, -1, keepdims=True)
    centered = rows - mean
    inv_std = lax.rsqrt(jnp.mean(centered * centered, -1, keepdims=True) + eps_norm)
    return centered * inv_std, inv_std


def norm_back(grad_rows, unit_rows, inv_std, gain):
    scaled = grad_rows * gain
    return inv_std * (
        scaled
        - jnp.mean(scaled, -1, keepdims=True)
        - unit_rows * jnp.mean(scaled * unit_rows, -1, keepdims=True)
    )


def gelu_pair(rows):
    size = jnp.abs(rows)
    t = 1.0 / (1.0 + (0.3275911 * root_half) * size)
    bell = jnp.exp2(rows * rows * (-0.5 * log2_e))
    poly = (
        (((0.5 * 1.061405429 * t - 0.5 * 1.453152027) * t + 0.5 * 1.421413741) * t - 0.5 * 0.284496736)
        * t
        + 0.5 * 0.254829592
    ) * t
    tail = poly * bell
    upper = jnp.where(rows < 0.0, tail, 1.0 - tail)
    return rows * upper, upper + rows * bell * inv_root_two_pi


def head_masks(width):
    heads = lax.broadcasted_iota(jnp.int32, (1, width), 1) // HD
    return [jnp.where(heads == h, 1.0, 0.0).astype(BF16) for h in range(width // HD)]


def expand(rows):
    masks = head_masks(rows.shape[1])
    return jnp.concatenate([rows * mask for mask in masks], 0)


def collapse(stacked):
    width = stacked.shape[1]
    lanes = lax.broadcasted_iota(jnp.int32, (CELLS, width), 1)
    total = stacked[:CELLS]
    for h in range(1, width // HD):
        total = jnp.where(lanes >= h * HD, stacked[h * CELLS : (h + 1) * CELLS], total)
    return total


def split(rows):
    return rows[:, :LANES_A], rows[:, LANES_A:]


def attend(queries, keys, values, bias):
    q_a, q_b = split(queries)
    k_a, k_b = split(keys)
    v_a, v_b = split(values)
    scores = jnp.concatenate([nt(k_a, expand(q_a)), nt(k_b, expand(q_b))], 1)
    scores = scores * (scale * log2_e) + bias
    exponent = jnp.exp2(scores - jnp.max(scores, 0, keepdims=True))
    probs = exponent * (1.0 / jnp.sum(exponent, 0, keepdims=True))
    low = probs.astype(BF16)
    mixed = jnp.concatenate(
        [collapse(tn(low[:, :COLS_A], v_a)), collapse(tn(low[:, COLS_A:], v_b))], 1
    )
    return mixed.astype(BF16), probs


def attend_back(queries, keys, values, probs, grad_mixed):
    q_a, q_b = [expand(part) for part in split(queries)]
    k_a, k_b = split(keys)
    v_a, v_b = split(values)
    g_a, g_b = [expand(part) for part in split(grad_mixed)]
    d_probs = jnp.concatenate([nt(v_a, g_a), nt(v_b, g_b)], 1)
    d_scores = probs * (d_probs - jnp.sum(d_probs * probs, 0, keepdims=True))
    low = probs.astype(BF16)
    low_d = d_scores.astype(BF16)
    d_values = jnp.concatenate([nn(low[:, :COLS_A], g_a), nn(low[:, COLS_A:], g_b)], 1)
    d_keys = jnp.concatenate([nn(low_d[:, :COLS_A], q_a), nn(low_d[:, COLS_A:], q_b)], 1) * scale
    d_queries = (
        jnp.concatenate(
            [collapse(tn(low_d[:, :COLS_A], k_a)), collapse(tn(low_d[:, COLS_A:], k_b))], 1
        )
        * scale
    )
    return d_queries, d_keys, d_values, d_scores


def with_ones(rows):
    return jnp.concatenate([rows.T, jnp.ones((16, rows.shape[0]), BF16)], 0)


def col_sum(rows):
    return jnp.sum(rows, 0, keepdims=True)


def start_sums(first, old_refs, new_refs):
    @pl.when(pl.program_id(0) == 0)
    def _():
        for k, new in enumerate(new_refs):
            new[...] = jnp.zeros_like(new) if first else old_refs[k][...]


def restore(matrix, rows):
    high = rows.astype(BF16)
    low = (rows - high.astype(F32)).astype(BF16)
    return tn(matrix, high) + tn(matrix, low)


CHUNK = 256


def encoder_forward(
    core_ref, tok, order, vec, w_qkv, b_qkv, bias, w_out, w_up, b_up, w_down,
    send, keep, n1_out, n2_out, rs_out, qkv_out, p_out, o_out, a_out, s_out,
):
    rows_z = tok.shape[3]
    size = 4 * rows_z
    pieces = []
    for x in range(2):
        for y in range(2):
            part = tok[0, 2 * x : 2 * x + 2, 2 * y : 2 * y + 2].reshape(size, -1)
            pieces.append(nn(order[...], part))
    entry = windows_of(jnp.stack(pieces))
    unit, inv_std = normalize(entry)
    n1_out[0] = unit
    rs_out[0, :, :128] = jnp.broadcast_to(inv_std, (entry.shape[0], 128))
    left = (unit * vec[0:1] + vec[1:2]).astype(BF16)
    triple = nn(left, w_qkv[...]) + b_qkv[...]
    qkv_out[0] = triple.astype(BF16)
    for k in range(entry.shape[0] // CELLS):
        rows = slice(k * CELLS, (k + 1) * CELLS)
        mixed, probs = attend(
            qkv_out[0, rows, 0:192], qkv_out[0, rows, 256:448], qkv_out[0, rows, 512:704], bias[...]
        )
        p_out[0, k] = probs
        o_out[0, rows] = mixed
    middle = entry + nn(o_out[0], w_out[...]) + vec[4:5]
    unit, inv_std = normalize(middle)
    n2_out[0] = unit
    rs_out[0, :, 128:] = jnp.broadcast_to(inv_std, (entry.shape[0], 128))
    left = (unit * vec[2:3] + vec[3:4]).astype(BF16)
    results = []
    for k in range(entry.shape[0] // CHUNK):
        rows = slice(k * CHUNK, (k + 1) * CHUNK)
        hidden, slope = gelu_pair(nn(left[rows], w_up[...]) + b_up[...])
        hidden = hidden.astype(BF16)
        a_out[0, rows] = hidden
        s_out[0, rows] = slope
        results.append(nn(hidden, w_down[...]))
    result = middle + jnp.concatenate(results, 0) + vec[5:6]
    for field, rows in enumerate((result, triple[:, 256:448], triple[:, 512:704])):
        rolled = roll_rows(pieces_of(rows), 8).astype(BF16)
        send[0, :, field] = rolled[:2]
        keep[0, :, field] = rolled[2:]


def mlp_back(grad, grad_low, hidden, slope, left_two, unit, inv_std, w_up, w_down, vec, sums):
    g_up, g_down, g_vec = sums
    backs = []
    total_up = None
    turned = grad_low.T
    ones = with_ones(left_two)
    for k in range(grad.shape[0] // CHUNK):
        rows = slice(k * CHUNK, (k + 1) * CHUNK)
        d_pre = (nt(grad_low[rows], w_down[...]) * slope(rows)).astype(BF16)
        part = nn(ones[:, rows], d_pre)
        total_up = part if total_up is None else total_up + part
        backs.append(nt(d_pre, w_up[...]))
    g_up[...] += total_up
    g_down[...] += nn(turned, hidden)
    d_normed = jnp.concatenate(backs, 0)
    g_vec[2:3] += col_sum(d_normed * unit)
    g_vec[3:4] += col_sum(d_normed)
    g_vec[4:5] += col_sum(grad)
    return grad + norm_back(d_normed, unit, inv_std, vec[2:3])


def encoder_backward(
    first, order, vec, w_qkv, w_out, w_up, w_down,
    keep_a, keep_b, recv_a, recv_b,
    n1_in, n2_in, rs_in, qkv_in, p_in, o_in, a_in, s_in, *rest,
):
    old, (out, *sums, dqkv) = ([], rest) if first else (rest[:6], rest[6:])
    g_up, g_down, g_qkv, g_out, g_vec, g_bias = sums
    start_sums(first, old, sums)
    fields = []
    for field in range(3):
        pieces = jnp.stack(
            [recv_b[0, 0, field], recv_a[0, 0, field], keep_b[0, 0, field], keep_a[0, 0, field]]
        )
        fields.append(windows_of(pieces))
    grad_low, d_key_1, d_value_1 = fields
    grad = grad_low.astype(F32)
    unit_1, unit_2 = n1_in[0], n2_in[0]
    wide_1, wide_2 = [
        jnp.concatenate([r, r[:, :64]], 1) for r in (rs_in[0, :, :128], rs_in[0, :, 128:])
    ]
    left_1 = (unit_1 * vec[0:1] + vec[1:2]).astype(BF16)
    left_2 = (unit_2 * vec[2:3] + vec[3:4]).astype(BF16)
    d_middle = mlp_back(
        grad, grad_low, a_in[0], lambda rows: s_in[0, rows], left_2, unit_2, wide_2, w_up, w_down, vec,
        (g_up, g_down, g_vec),
    )
    branch = d_middle.astype(BF16)
    g_out[...] += nn(with_ones(o_in[0]), branch)
    d_mixed = nt(branch, w_out[...]).astype(BF16)
    d_table = None
    for k in range(grad.shape[0] // CELLS):
        rows = slice(k * CELLS, (k + 1) * CELLS)
        d_q, d_k, d_v, d_s = attend_back(
            qkv_in[0, rows, 0:192], qkv_in[0, rows, 256:448], qkv_in[0, rows, 512:704],
            p_in[0, k], d_mixed[rows],
        )
        dqkv[0, rows] = d_q.astype(BF16)
        dqkv[1, rows] = (d_k + d_key_1[rows].astype(F32)).astype(BF16)
        dqkv[2, rows] = (d_v + d_value_1[rows].astype(F32)).astype(BF16)
        d_table = d_s if d_table is None else d_table + d_s
    g_bias[...] += d_table
    ones = with_ones(left_1)
    d_normed = None
    for field in range(3):
        cols = slice(field * 256, field * 256 + 192)
        g_qkv[:, cols] += nn(ones, dqkv[field])
        part = nt(dqkv[field], w_qkv[:, cols])
        d_normed = part if d_normed is None else d_normed + part
    g_vec[0:1] += col_sum(d_normed * unit_1)
    g_vec[1:2] += col_sum(d_normed)
    result = pieces_of(d_middle + norm_back(d_normed, unit_1, wide_1, vec[0:1]))
    rows_z = out.shape[2]
    for x in range(2):
        for y in range(2):
            part = restore(order[...], result[2 * x + y])
            out[2 * x : 2 * x + 2, 2 * y : 2 * y + 2] = part.reshape(2, 2, rows_z, -1)


def decoder(
    first, core_ref, order, vec, w_q, b_q, bias, w_out, w_up, b_up, w_down,
    keep_1, keep_0, recv_1, recv_0, cot_1, cot_0, cot_r1, cot_r0, *rest,
):
    old, new = ([], rest) if first else (rest[:6], rest[6:])
    out, own, halo, *sums, p_scr, o_scr, a_scr, s_scr, dqkv = new
    g_up, g_down, g_q, g_out, g_vec, g_bias = sums
    start_sums(first, old, sums)
    fields = []
    for field in range(3):
        pieces = jnp.stack([ref[0, 0, field] for ref in (keep_1, keep_0, recv_1, recv_0)])
        fields.append(windows_of(pieces))
    entry_low, keys, values = fields
    entry = entry_low.astype(F32)
    unit_1, inv_1 = normalize(entry)
    left_1 = (unit_1 * vec[0:1] + vec[1:2]).astype(BF16)
    queries = (nn(left_1, w_q[...]) + b_q[...]).astype(BF16)
    windows = entry.shape[0] // CELLS
    for k in range(windows):
        rows = slice(k * CELLS, (k + 1) * CELLS)
        mixed, probs = attend(
            queries[rows], keys[rows], values[rows], bias[0, 1 if k == windows - 1 else 0]
        )
        p_scr[k] = probs
        o_scr[rows] = mixed
    middle = entry + nn(o_scr[...], w_out[...]) + vec[4:5]
    unit_2, inv_2 = normalize(middle)
    left_2 = (unit_2 * vec[2:3] + vec[3:4]).astype(BF16)
    results = []
    for k in range(entry.shape[0] // CHUNK):
        rows = slice(k * CHUNK, (k + 1) * CHUNK)
        hidden, slope = gelu_pair(nn(left_2[rows], w_up[...]) + b_up[...])
        hidden = hidden.astype(BF16)
        a_scr[rows] = hidden
        s_scr[rows] = slope
        results.append(nn(hidden, w_down[...]))
    result = pieces_of(middle + jnp.concatenate(results, 0) + vec[5:6])
    rows_z = out.shape[2]
    size = 4 * rows_z
    for x in range(2):
        for y in range(2):
            part = restore(order[...], result[2 * x + y])
            out[2 * x : 2 * x + 2, 2 * y : 2 * y + 2] = part.reshape(2, 2, rows_z, -1)

    cots = [
        nn(order[...], ref[0].reshape(size, -1)).astype(BF16) for ref in (cot_1, cot_0, cot_r1, cot_r0)
    ]
    grad_low = windows_of(jnp.stack(cots))
    grad = grad_low.astype(F32)
    d_middle = mlp_back(
        grad, grad_low, a_scr[...], lambda rows: s_scr[rows], left_2, unit_2, inv_2, w_up, w_down, vec,
        (g_up, g_down, g_vec),
    )
    branch = d_middle.astype(BF16)
    g_out[...] += nn(with_ones(o_scr[...]), branch)
    d_mixed = nt(branch, w_out[...]).astype(BF16)
    d_table = None
    for k in range(windows):
        rows = slice(k * CELLS, (k + 1) * CELLS)
        d_q, d_k, d_v, d_s = attend_back(
            queries[rows], keys[rows], values[rows], p_scr[k], d_mixed[rows]
        )
        dqkv[0, rows] = d_q
        dqkv[1, rows] = d_k
        dqkv[2, rows] = d_v
        d_table = d_s if d_table is None else d_table + d_s
    g_bias[...] += d_table
    d_queries = dqkv[0].astype(BF16)
    g_q[...] += nn(with_ones(left_1), d_queries)
    d_normed = nt(d_queries, w_q[...])
    g_vec[0:1] += col_sum(d_normed * unit_1)
    g_vec[1:2] += col_sum(d_normed)
    d_entry = d_middle + norm_back(d_normed, unit_1, inv_1, vec[0:1])
    for field, rows in enumerate((d_entry, dqkv[1], dqkv[2])):
        turned = roll_rows(pieces_of(rows), size - 8).astype(BF16)
        own[0, :, field] = turned[:2]
        halo[0, :, field] = turned[2:]


def whole(array):
    zeros = (0,) * array.ndim
    return pl.BlockSpec(array.shape, lambda *_: zeros)


def sums_shapes(channels, hidden, q_cols):
    return [
        jax.ShapeDtypeStruct(shape, F32)
        for shape in (
            (channels + 16, hidden),
            (channels, hidden),
            (channels + 16, q_cols),
            (channels + 16, channels),
            (8, channels),
            (CELLS, HEADS * CELLS),
        )
    ]


def cost(cells, per_cell, hbm):
    return pl.CostEstimate(
        flops=2 * cells * per_cell, bytes_accessed=hbm, transcendentals=cells * 1536
    )


params = pltpu.CompilerParams(
    dimension_semantics=("arbitrary",), vmem_limit_bytes=VMEM_BYTES
)


def run_encoder(core, tokens, batch, consts):
    _, _, rows_y, rows_z, channels = tokens.shape
    groups, size = rows_y // WIN, 4 * rows_z
    cells, windows = 4 * size, rows_z // WIN
    hidden = consts[6].shape[1]
    slab = jax.ShapeDtypeStruct((groups, 2, 3, size, channels), BF16)
    outs = [
        slab,
        slab,
        jax.ShapeDtypeStruct((groups, cells, channels), F32),
        jax.ShapeDtypeStruct((groups, cells, channels), F32),
        jax.ShapeDtypeStruct((groups, cells, 256), F32),
        jax.ShapeDtypeStruct((groups, cells, 768), BF16),
        jax.ShapeDtypeStruct((groups, windows, CELLS, HEADS * CELLS), F32),
        jax.ShapeDtypeStruct((groups, cells, channels), BF16),
        jax.ShapeDtypeStruct((groups, cells, hidden), BF16),
        jax.ShapeDtypeStruct((groups, cells, hidden), F32),
    ]

    def row(array):
        zeros = (0,) * (array.ndim - 1)
        return pl.BlockSpec((1, *array.shape[1:]), lambda i, c: (i, *zeros))

    return pl.pallas_call(
        encoder_forward,
        grid_spec=pltpu.PrefetchScalarGridSpec(
            num_scalar_prefetch=1,
            grid=(groups,),
            in_specs=[
                pl.BlockSpec(
                    (1, WIN, WIN, rows_z, channels), lambda i, c: (batch, c[0], i, 0, 0)
                ),
                *[whole(a) for a in consts],
            ],
            out_specs=[row(a) for a in outs],
        ),
        out_shape=outs,
        compiler_params=params,
        cost_estimate=cost(groups * cells, 466944, groups * cells * 7500),
        name="encoder_forward",
    )(core, tokens, *consts)


def run_encoder_back(own, halo, saved, old, consts, rows_z):
    groups, _, _, size, channels = own.shape
    hidden = consts[4].shape[1]
    first = old is None
    shapes = sums_shapes(channels, hidden, 768)
    outs = [jax.ShapeDtypeStruct((WIN, groups * WIN, rows_z, channels), F32), *shapes]

    def slab(unit):
        def place(i):
            return ((i if unit == 0 else (i + groups - 1) % groups), unit, 0, 0, 0)

        return pl.BlockSpec((1, 1, 3, size, channels), place)

    def row(array):
        zeros = (0,) * (array.ndim - 1)
        return pl.BlockSpec((1, *array.shape[1:]), lambda i: (i, *zeros))

    olds = [] if first else list(old)
    return pl.pallas_call(
        functools.partial(encoder_backward, first),
        grid=(groups,),
        in_specs=[
            *[whole(a) for a in consts],
            slab(0),
            slab(1),
            slab(0),
            slab(1),
            *[row(a) for a in saved],
            *[whole(a) for a in olds],
        ],
        out_specs=[
            pl.BlockSpec((WIN, WIN, rows_z, channels), lambda i: (0, i, 0, 0)),
            *[whole(a) for a in shapes],
        ],
        out_shape=outs,
        scratch_shapes=[pltpu.VMEM((3, 4 * size, channels), BF16)],
        compiler_params=params,
        cost_estimate=cost(groups * 4 * size, 933888, groups * 4 * size * 9000),
        name="encoder_backward",
    )(*consts, own, own, halo, halo, *saved, *olds)


def run_decoder(core, keep, recv, cotangent, cot_recv, batch, old, consts):
    groups, _, _, size, channels = keep.shape
    rows_z = size // 4
    hidden = consts[6].shape[1]
    windows = rows_z // WIN
    first = old is None
    shapes = sums_shapes(channels, hidden, channels)
    slab_shape = jax.ShapeDtypeStruct((groups, 2, 3, size, channels), BF16)
    outs = [
        jax.ShapeDtypeStruct((WIN, groups * WIN, rows_z, channels), F32),
        slab_shape,
        slab_shape,
        *shapes,
    ]

    def slab(unit):
        def place(i, c):
            return ((i if unit == 1 else (i + 1) % groups), unit, 0, 0, 0)

        return pl.BlockSpec((1, 1, 3, size, channels), place)

    def cot(unit, own):
        def place(i, c):
            y = 2 * i + 1 if unit == 1 else (2 * i + 2) % (2 * groups)
            return (batch, 2 * c[0] + 1 if own else 0, y, 0, 0)

        return pl.BlockSpec((1, 2, 2, rows_z, channels), place)

    def bias_place(i, c):
        return (i // (groups - 1), 0, 0, 0)

    specs = [whole(a) for a in consts]
    specs[4] = pl.BlockSpec((1, *consts[4].shape[1:]), bias_place)
    olds = [] if first else list(old)
    out_slab = pl.BlockSpec((1, 2, 3, size, channels), lambda i, c: (i, 0, 0, 0, 0))
    return pl.pallas_call(
        functools.partial(decoder, first),
        grid_spec=pltpu.PrefetchScalarGridSpec(
            num_scalar_prefetch=1,
            grid=(groups,),
            in_specs=[
                *specs,
                slab(1),
                slab(0),
                slab(1),
                slab(0),
                cot(1, True),
                cot(0, True),
                cot(1, False),
                cot(0, False),
                *[whole(a) for a in olds],
            ],
            out_specs=[
                pl.BlockSpec((WIN, WIN, rows_z, channels), lambda i, c: (0, i, 0, 0)),
                out_slab,
                out_slab,
                *[whole(a) for a in shapes],
            ],
            scratch_shapes=[
                pltpu.VMEM((windows, CELLS, HEADS * CELLS), F32),
                pltpu.VMEM((4 * size, channels), BF16),
                pltpu.VMEM((4 * size, hidden), BF16),
                pltpu.VMEM((4 * size, hidden), F32),
                pltpu.VMEM((3, 4 * size, channels), F32),
            ],
        ),
        out_shape=outs,
        compiler_params=params,
        cost_estimate=cost(groups * 4 * size, 1253376, groups * 4 * size * 4000),
        name="decoder",
    )(core, *consts, keep, keep, recv, recv, cotangent, cotangent, cot_recv, cot_recv, *olds)


def body(
    tokens,
    cotangent,
    ln1_gain,
    ln1_bias,
    q_weight,
    q_bias,
    kv_weight,
    v_bias,
    out_weight,
    out_bias,
    rel_table,
    ln2_gain,
    ln2_bias,
    up_weight,
    up_bias,
    down_weight,
    down_bias,
):
    batches, planes, rows_y, rows_z, channels = tokens.shape
    axes = ("section", "tok")
    core = lax.axis_index("section")
    block = lax.axis_index("tok")
    blocks = lax.axis_size("tok")
    is_encoder = core == 0
    core_arg = core.astype(jnp.int32).reshape(1)

    def device(position):
        position = position % (2 * blocks)
        return (position % 2) * blocks + position // 2

    to_previous = [(device(r), device(r - 1)) for r in range(2 * blocks)]
    to_next = [(device(r), device(r + 1)) for r in range(2 * blocks)]

    def both(array):
        return lax.all_gather(array, "section", axis=0, tiled=True)

    vec = jnp.concatenate(
        [
            v.astype(F32)[:, None]
            for v in map(both, (ln1_gain, ln1_bias, ln2_gain, ln2_bias, out_bias, down_bias))
        ],
        1,
    )
    vec = jnp.pad(vec, ((0, 0), (0, 2), (0, 0)))
    w_q, w_out, w_up, w_down = map(both, (q_weight, out_weight, up_weight, down_weight))
    b_q, b_up, table = map(both, (q_bias, up_bias, rel_table))
    b_up = b_up.astype(F32)[:, None]
    b_q = b_q.astype(F32)[:, None]
    pad = ((0, 0), (0, 256 - channels))
    w_qkv = jnp.concatenate(
        [
            jnp.pad(w, pad)
            for w in (w_q[0], kv_weight[:, :channels], kv_weight[:, channels:])
        ],
        1,
    )
    b_qkv = jnp.concatenate(
        [
            jnp.pad(b, pad)
            for b in (b_q[0], jnp.zeros((1, channels), F32), v_bias.astype(F32)[None])
        ],
        1,
    )
    index = relative_index()
    one_hot = (
        jnp.asarray(index.reshape(-1))[None, :] == jnp.arange(SPAN**3)[:, None]
    ).astype(F32)
    bias = jnp.dot(
        table.astype(F32).reshape(2 * HEADS, -1), one_hot, precision=lax.Precision.HIGHEST
    ).reshape(2, HEADS, CELLS, CELLS)
    bias = bias.transpose(0, 2, 1, 3) * log2_e
    bias_enc = bias[0].reshape(CELLS, HEADS * CELLS)
    units = np.stack([np.arange(CELLS) // 32, np.arange(CELLS) // 16 % 2, np.arange(CELLS) // 8 % 2])
    differ = units[:, :, None] != units[:, None, :]
    is_last = (core == 1) & (block == blocks - 1)
    apart = (
        (is_last & jnp.asarray(differ[0]))[None, None]
        | jnp.asarray(np.arange(2)[:, None, None, None] * differ[1] > 0)
        | jnp.asarray(np.arange(2)[None, :, None, None] * differ[2] > 0)
    )
    mask = jnp.where(apart, mask_fill * log2_e, 0.0).astype(F32)
    bias_dec = (bias[1][None, None] + mask[:, :, :, None, :]).reshape(
        2, 2, CELLS, HEADS * CELLS
    )
    order = jnp.asarray(order_matrix(rows_z, 0), BF16)
    order_rolled = jnp.asarray(order_matrix(rows_z, 1), BF16)

    half = lax.dynamic_slice_in_dim(cotangent, core * WIN, SHIFT, 1)
    cot_recv = lax.ppermute(half, axes, to_previous)

    enc_consts = (order, vec[0], w_qkv, b_qkv, bias_enc, w_out[0], w_up[0], b_up[0], w_down[0])
    enc_back_consts = (order, vec[0], w_qkv, w_out[0], w_up[0], w_down[0])
    dec_consts = (
        order_rolled, vec[1], w_q[1], b_q[1], bias_dec, w_out[1], w_up[1], b_up[1], w_down[1],
    )

    handed, saved = [], []
    for batch in range(batches):
        send, keep, *rest = run_encoder(core_arg, tokens, batch, enc_consts)
        handed.append((keep, lax.ppermute(send, axes, to_previous)))
        saved.append(rest)
    dec_sums = None
    returned, outputs, sib_outputs, halo_outputs = [], [], [], []
    to_decoder = [(t, blocks + t) for t in range(blocks)]
    to_encoder = [(blocks + t, t) for t in range(blocks)]
    to_after = [(blocks + t, blocks + (t + 1) % blocks) for t in range(blocks)]
    for batch in range(batches):
        out, own, halo, *dec_sums = run_decoder(
            core_arg, *handed[batch], cotangent, cot_recv, batch, dec_sums, dec_consts
        )
        returned.append((own, lax.ppermute(halo, axes, to_next)))
        outputs.append(out)
        halo_outputs.append(lax.ppermute(out[SHIFT:], axes, to_after))
        sib_outputs.append(lax.ppermute(out, axes, to_decoder))
    enc_sums = None
    grads, sib_grads = [], []
    for batch in range(batches):
        out, *enc_sums = run_encoder_back(
            *returned[batch], saved[batch], enc_sums, enc_back_consts, rows_z
        )
        grads.append(out)
        sib_grads.append(lax.ppermute(out, axes, to_encoder))

    ends = jnp.stack(
        [
            jnp.where(
                is_encoder,
                jnp.concatenate([grads[b], sib_grads[b]], 0),
                jnp.roll(
                    jnp.concatenate([halo_outputs[b], sib_outputs[b], outputs[b][:SHIFT]], 0),
                    SHIFT,
                    1,
                ),
            )
            for b in range(batches)
        ]
    )[None]

    def pack(sums):
        s_up, s_down, s_q, s_out, s_vec, s_bias = sums
        s_table = jnp.dot(
            s_bias.reshape(CELLS, HEADS, CELLS).transpose(1, 0, 2).reshape(HEADS, -1),
            one_hot.T,
            precision=lax.Precision.HIGHEST,
        )
        return [s_up, s_down, s_q[:, :channels], s_out, s_vec, s_table]

    enc_grads, dec_grads = pack(enc_sums), pack(dec_sums)
    kv_sums = jnp.concatenate([enc_sums[2][:, 256:448], enc_sums[2][:, 512:704]], 1)

    def flat(arrays):
        return jnp.concatenate([a.reshape(-1) for a in arrays])

    flat_enc, flat_dec = flat(enc_grads), flat(dec_grads)
    mine = jnp.where(is_encoder, flat_enc, flat_dec)
    theirs = jnp.where(is_encoder, flat_dec, flat_enc)
    swapped = lax.ppermute(theirs, "section", [(0, 1), (1, 0)])
    kv_flat = kv_sums.reshape(-1)
    kv_swapped = lax.ppermute(kv_flat, "section", [(0, 1), (1, 0)])
    total = lax.psum(jnp.concatenate([mine + swapped, kv_flat + kv_swapped]), "tok")
    parts, start = [], 0
    for array in [*enc_grads, kv_sums]:
        parts.append(total[start : start + array.size].reshape(array.shape))
        start += array.size
    t_up, t_down, t_q, t_out, t_vec, t_table, t_kv = parts
    return (
        ends,
        t_vec[0:1],
        t_vec[1:2],
        t_q[None, :channels],
        t_q[channels : channels + 1],
        t_kv[None, :channels],
        t_kv[channels : channels + 1, channels:],
        t_out[None, :channels],
        t_out[channels : channels + 1],
        t_table[None],
        t_vec[2:3],
        t_vec[3:4],
        t_up[None, :channels],
        t_up[channels : channels + 1],
        t_down.T[None],
        t_vec[4:5],
    )


def solution(mesh):
    in_specs = (
        P(None, "tok", None, None, None),
        P(None, "tok", None, None, None),
        P("section", None),
        P("section", None),
        P("section", None, None),
        P("section", None),
        P(),
        P(),
        P("section", None, None),
        P("section", None),
        P("section", None, None),
        P("section", None),
        P("section", None),
        P("section", None, None),
        P("section", None),
        P("section", None, None),
        P("section", None),
    )
    out_specs = (
        P("section", None, "tok", None, None, None),
        P("section", None),
        P("section", None),
        P("section", None, None),
        P("section", None),
        P("section", None, None),
        P("section", None),
        P("section", None, None),
        P("section", None),
        P("section", None, None),
        P("section", None),
        P("section", None),
        P("section", None, None),
        P("section", None),
        P("section", None, None),
        P("section", None),
    )
    return jax.shard_map(body, mesh=mesh, in_specs=in_specs, out_specs=out_specs, check_vma=False)
```

time: 2590 us -> 574 us (0.22)
  local copies, waits for them, and re-layouts: 1120 us -> 75.3 us
  matrix products: 452 us -> 6.59 us
  other arithmetic: 410 us -> 42.6 us
  waiting for transfers between devices: 420 us -> 122 us
  Pallas kernels: 0 us -> 247 us
  blocking collectives: 117 us -> 26.7 us
    dot_general x84 -> x3, matrix products: 452 us -> 6.59 us  [the longest x2 4.87 us: pack(): jnp.dot(s_bias.reshape(CELLS, HEADS, CELLS).transpose(1, 0, 2).reshape(HE...]
    another operation x42 -> x2, local copies, waits for them, and re-layouts: 370 us -> 1.43 us  [the longest x1 0.74 us: body(): bias_enc = bias[0].reshape(CELLS, HEADS * CELLS)]
    ppermute x18, waiting for transfers between devices: 294 us -> 22.9 us  [the longest x3 16.4 us: body(): returned.append((own, lax.ppermute(halo, axes, to_next)))]
    pallas_call x0 -> x9, Pallas kernels: none -> 247 us  [the longest x3 110 us: run_decoder(): pl.pallas_call(functools.partial(decoder, first), grid_spec=pltpu.Prefetc...]
    convert_element_type x35 -> x0, local copies, waits for them, and re-layouts: 246 us -> none  [the longest x16 123 us: body(): from_windows(d_query_win, planes, rows_y, rows_z).astype(jnp.bfloat16)]
    convert_element_type x21 -> x2, other arithmetic: 142 us -> 0.01 us  [the longest x1 0.01 us: body(): b_up = b_up.astype(F32)[:, None]]
    reshape x44 -> x20, local copies, waits for them, and re-layouts: 132 us -> 11 us  [the longest x12 7.78 us: flat(): return jnp.concatenate([a.reshape(-1) for a in arrays])]
    reduce_sum x28 -> x0, other arithmetic: 119 us -> none  [the longest x4 44.1 us: attend_back(): jnp.sum(d_scores, 0, dtype=jnp.float32)]
  transfers between devices with their start and end apart: 20 -> 19, of which waited for: 13 -> 3; matrix products, arithmetic and copies ran while one was open for 9% -> 17% of each run, Pallas kernels for 0% -> 40%
where the time goes in v1:
time: 574 us; the launch traced here: 565 us
  Pallas kernels  247 us (43%)
  waiting for transfers between devices  122 us (21%)
  local copies, waits for them, and re-layouts  75.3 us (13%)
  other arithmetic  42.6 us (7%)
  starting transfers between devices  29.1 us (5%)
  blocking collectives  26.7 us (5%)
  between operations  15.2 us (3%)
  matrix products  6.59 us (1%)
    pallas_call x3, Pallas kernels, run_decoder(): pl.pallas_call(functools.partial(decoder, first), grid_spec=pltpu.Prefetc...  110 us
    psum x1, waiting for transfers between devices, body(): lax.psum(jnp.concatenate([mine + swapped, kv_flat + kv_swapped]), 'tok')  99.4 us
    pallas_call x3, Pallas kernels, run_encoder_back(): pl.pallas_call(functools.partial(encoder_backward, first), grid=(groups,)...  70.8 us
    pallas_call x3, Pallas kernels, run_encoder(): pl.pallas_call(encoder_forward, grid_spec=pltpu.PrefetchScalarGridSpec(nu...  66.1 us
    all_gather x13, blocking collectives, both(): return lax.all_gather(array, 'section', axis=0, tiled=True)  26.7 us
    ppermute x3, waiting for transfers between devices, body(): returned.append((own, lax.ppermute(halo, axes, to_next)))  16.4 us
    select_n x3, other arithmetic, body(): jnp.where(is_encoder, jnp.concatenate([grads[b], sib_grads[b]], 0), jnp.r...  13.6 us
  transfers between devices with their start and end apart: 19, of which 3 were waited for; matrix products, arithmetic and copies ran while one was open for 17% of the time, Pallas kernels for 40%

profile of v1, /device:TPU:0, one launch (start us, length us, event | category | flops | bytes accessed | tf_op | source)
XLA Modules:
  0.0 564.6 jit_solution(17696928273572163500)
XLA Ops:
  7.9 2.1 all-gather
  10.0 2.0 all-gather.1
  12.0 2.0 all-gather.6
  14.6 2.0 all-gather.4
  16.6 2.0 all-gather.2
  18.6 2.0 all-gather.3
  20.5 2.0 all-gather.5
  22.5 1.9 all-gather.7
  25.7 2.0 all_gather.50
  29.6 2.2 all_gather.45
  32.5 2.1 all_gather.46
  35.3 1.7 fusion.4
  38.2 2.2 all_gather.47
  41.3 2.2 all_gather.48
  45.8 22.0 %encoder_forward.3 = (bf16[4,2,3,128,192]{4,3,2,1,0:T(8,128)(2,1)}, bf16[4,2,3,128,192]{4,3,2,1,0:T(8,128)(2,1)}, f32[4,512,192]{2,1,0:T(8,128)}, f32[4,512,192]...) custom-call(s32[1]{0:T(128)} %bitcast.11.core_ref, ...), custom_call_target="tpu_custom_call" | custom-call | flops 1912602624 | bytes 15360000 | tf_op jit(solution)/shard_map/encoder_forward/pallas_call | solution.py:461
  67.8 2.6 copy.71
  70.4 6.6 %collective-permute-start = (bf16[4,2,3,128,192]{3,4,2,1,0:T(8,128)(2,1)}, bf16[4,2,3,128,192]{3,4,2,1,0:T(8,128)(2,1)}, u32[]{:S(2)}, u32[]{:S(2)}) collective-permute-start(bf16[4,2,3,128,192]{3,4,2,1,0:T(8,128)(2,1)} %copy.71), channel_id=1, source_target_pairs={{0,31},{16,0},{1,16},{17,1},{2,17},{18,2},{3,18},{19,3},{4,19},{20... | collective-permute-start | bytes 3538952 | tf_op jit(solution)/shard_map/ppermute | solution.py:696
  76.9 2.8 constant_dynamic-slice_fusion
  80.0 22.0 %encoder_forward.5 = (bf16[4,2,3,128,192]{4,3,2,1,0:T(8,128)(2,1)}, bf16[4,2,3,128,192]{4,3,2,1,0:T(8,128)(2,1)}, f32[4,512,192]{2,1,0:T(8,128)}, f32[4,512,192]...) custom-call(s32[1]{0:T(128)} %bitcast.11.core_ref, ...), custom_call_target="tpu_custom_call" | custom-call | flops 1912602624 | bytes 15360000 | tf_op jit(solution)/shard_map/encoder_forward/pallas_call | solution.py:461
  102.1 2.5 copy.83
  105.1 22.1 %encoder_forward.4 = (bf16[4,2,3,128,192]{4,3,2,1,0:T(8,128)(2,1)}, bf16[4,2,3,128,192]{4,3,2,1,0:T(8,128)(2,1)}, f32[4,512,192]{2,1,0:T(8,128)}, f32[4,512,192]...) custom-call(s32[1]{0:T(128)} %bitcast.11.core_ref, ...), custom_call_target="tpu_custom_call" | custom-call | flops 1912602624 | bytes 15360000 | tf_op jit(solution)/shard_map/encoder_forward/pallas_call | solution.py:461
  127.2 2.5 copy.77
  132.3 2.6 copy.72.recv_1.recv_0
  136.0 36.2 %decoder.3 = (f32[4,16,32,192]{3,2,1,0:T(8,128)}, bf16[4,2,3,128,192]{4,3,2,1,0:T(8,128)(2,1)}, bf16[4,2,3,128,192]{4,3,2,1,0:T(8,128)(2,1)}, f32[208,768]{1,0:T...) custom-call(s32[1]{0:T(128)} %bitcast.11.core_ref, ...), custom_call_target="tpu_custom_call" | custom-call | flops 5133828096 | bytes 8192000 | tf_op jit(solution)/shard_map/decoder/pallas_call | solution.py:558
  172.2 2.5 copy.74
  174.9 5.0 collective-permute-start.5
  179.9 2.6 copy.84.recv_1.recv_0
  182.6 2.5 copy.78.recv_1.recv_0
  185.1 36.7 %decoder.4 = (f32[4,16,32,192]{3,2,1,0:T(8,128)}, bf16[4,2,3,128,192]{4,3,2,1,0:T(8,128)(2,1)}, bf16[4,2,3,128,192]{4,3,2,1,0:T(8,128)(2,1)}, f32[208,768]{1,0:T...) custom-call(s32[1]{0:T(128)} %bitcast.11.core_ref, ...), custom_call_target="tpu_custom_call" | custom-call | flops 5133828096 | bytes 8192000 | tf_op jit(solution)/shard_map/decoder/pallas_call | solution.py:558
  221.9 37.0 %decoder.5 = (f32[4,16,32,192]{3,2,1,0:T(8,128)}, bf16[4,2,3,128,192]{4,3,2,1,0:T(8,128)(2,1)}, bf16[4,2,3,128,192]{4,3,2,1,0:T(8,128)(2,1)}, f32[208,768]{1,0:T...) custom-call(s32[1]{0:T(128)} %bitcast.11.core_ref, ...), custom_call_target="tpu_custom_call" | custom-call | flops 5133828096 | bytes 8192000 | tf_op jit(solution)/shard_map/decoder/pallas_call | solution.py:558
  263.0 2.4 fusion
  265.8 2.6 copy.86
  268.3 2.5 copy.80
  271.2 2.8 copy.75.recv_a.recv_b
  273.9 16.4 %collective-permute-done.7 = bf16[4,2,3,128,192]{3,4,2,1,0:T(8,128)(2,1)} collective-permute-done((bf16[4,2,3,128,192]{3,4,2,1,0:T(8,128)(2,1)}, bf16[4,2,3,128,192]{3,4,2,1,0:T(8,128)(2,1)}, u32[]{:S(2)}, u32[]{:S(2)}) %collective-permute-start.7) | collective-permute-done | bytes 1179680 | tf_op jit(solution)/shard_map/ppermute | solution.py:707
  290.4 2.5 copy.81.recv_a.recv_b
  292.9 23.0 %encoder_backward.3 = (f32[4,16,32,192]{3,2,1,0:T(8,128)}, f32[208,768]{1,0:T(8,128)}, f32[192,768]{1,0:T(8,128)}, f32[208,768]{1,0:T(8,128)}, f32[208,192]{1,0:...) custom-call(bf16[128,128]{1,0:T(8,128)(2,1)} %constant.48.clone.order, f32[8,192]{1,0:T(8,128)} %get-tuple-element.203.vec, ...), custom_call_target="tpu_custom_call" | custom-call | flops 3825205248 | bytes 18432000 | tf_op jit(solution)/shard_map/encoder_backward/pallas_call | solution.py:499
  315.9 23.8 %encoder_backward.4 = (f32[4,16,32,192]{3,2,1,0:T(8,128)}, f32[208,768]{1,0:T(8,128)}, f32[192,768]{1,0:T(8,128)}, f32[208,768]{1,0:T(8,128)}, f32[208,192]{1,0:...) custom-call(bf16[128,128]{1,0:T(8,128)(2,1)} %constant.48.clone.order, f32[8,192]{1,0:T(8,128)} %get-tuple-element.203.vec, ...), custom_call_target="tpu_custom_call" | custom-call | flops 3825205248 | bytes 18432000 | tf_op jit(solution)/shard_map/encoder_backward/pallas_call | solution.py:499
  339.7 2.5 copy.87.recv_a.recv_b
  342.2 24.0 %encoder_backward.5 = (f32[4,16,32,192]{3,2,1,0:T(8,128)}, f32[208,768]{1,0:T(8,128)}, f32[192,768]{1,0:T(8,128)}, f32[208,768]{1,0:T(8,128)}, f32[208,192]{1,0:...) custom-call(bf16[128,128]{1,0:T(8,128)(2,1)} %constant.48.clone.order, f32[8,192]{1,0:T(8,128)} %get-tuple-element.203.vec, ...), custom_call_target="tpu_custom_call" | custom-call | flops 3825205248 | bytes 18432000 | tf_op jit(solution)/shard_map/encoder_backward/pallas_call | solution.py:499
  368.2 1.7 reshape.308
  371.0 2.4 fusion.1
  376.7 1.5 broadcast_select_fusion
  378.8 2.7 fusion.17
  381.5 1.6 collective-permute-start.4
  384.2 1.9 fusion.19
  386.4 3.3 collective-permute-start.15
  389.7 2.8 fusion.18
  392.4 2.7 collective-permute-start.10
  395.1 1.6 collective-permute-start.14
  396.8 1.6 collective-permute-start.9
  398.4 2.0 maximum_bitcast_fusion.3
  401.7 1.7 select_add_fusion
  404.7 1.6 collective-permute-start.8
  406.3 1.5 pad_maximum_fusion.6
  409.9 2.1 fusion.7
  412.0 2.1 fusion.5
  414.1 2.2 fusion.6
  416.3 3.2 maximum_select_fusion
  419.6 6.4 %collective-permute-done.13 = f32[4,16,32,192]{3,2,1,0:T(8,128)} collective-permute-done((f32[4,16,32,192]{3,2,1,0:T(8,128)}, f32[4,16,32,192]{3,2,1,0:T(8,128)}, u32[]{:S(2)}, u32[]{:S(2)}) %collective-permute-start.13) | collective-permute-done | bytes 1572896 | tf_op jit(solution)/shard_map/ppermute | solution.py:718
  426.0 5.2 maximum_select_fusion.2
  431.2 5.2 maximum_select_fusion.1
  436.4 10.7 %maximum_bitcast_fusion = f32[1,3,8,16,32,192]{5,4,3,2,1,0:T(8,128)} fusion(f32[1,8,16,32,192]{4,3,2,1,0:T(8,128)} %maximum_select_fusion.2, f32[1,8,16,32,192]{4,3,2,1,0:T(8,128)} %maximum_select_fusion.1, f32[1,8,16,32,192]{4,3,2,1,0:T(8,128)S(1)} %maximum_select_fusion), kind=kLoop, calls=%fused_computation | loop fusion | flops 4718592 | bytes 18874368 | tf_op jit(solution)/shard_map/broadcast_in_dim | solution.py:720
  447.1 99.4 %all-reduce.8.cloned.1.call-done = f32[470538]{0:T(1024)} async-done(((f32[470538]{0:T(1024)}), f32[470538]{0:T(1024)}) %all-reduce.8.cloned.1.call-update) | async-done | bytes 1882168 | tf_op jit(solution)/shard_map/psum | solution.py:756
  (149 shorter events, 43.1 us)
Async XLA Ops:
  7.2 539.3 %all-reduce.8.cloned.1.call-start = ((), (), s32[]{:S(2)}) async-start(), calls=%async_computation | async-start | bytes 3768320 | tf_op jit(solution)/shard_map/psum | solution.py:756
  35.3 2.9 copy-start.13
  37.2 4.1 copy-start.14
  70.4 61.9 %collective-permute-start = (bf16[4,2,3,128,192]{3,4,2,1,0:T(8,128)(2,1)}, bf16[4,2,3,128,192]{3,4,2,1,0:T(8,128)(2,1)}, u32[]{:S(2)}, u32[]{:S(2)}) collective-permute-start(bf16[4,2,3,128,192]{3,4,2,1,0:T(8,128)(2,1)} %copy.71), channel_id=1, source_target_pairs={{0,31},{16,0},{1,16},{17,1},{2,17},{18,2},{3,18},{19,3},{4,19},{20... | collective-permute-start | bytes 3538952 | tf_op jit(solution)/shard_map/ppermute | solution.py:696
  79.7 55.1 %collective-permute-start.1 = (bf16[3,2,16,32,192]{4,3,2,1,0:T(8,128)(2,1)}, bf16[3,2,16,32,192]{4,3,2,1,0:T(8,128)(2,1)S(1)}, u32[]{:S(2)}, u32[]{:S(2)}) collective-permute-start(bf16[3,2,16,32,192]{4,3,2,1,0:T(8,128)(2,1)} %constant_dynamic-slice_fusion), channel_id=1, source_target_pairs={{0,31},{16,0},{1,16},{17,1},{2,17},{18,2},{3,18},{19,3},{4,19},{20... | collective-permute-start | bytes 3538952 | tf_op jit(solution)/shard_map/ppermute | solution.py:685
  104.6 75.3 %collective-permute-start.11 = (bf16[4,2,3,128,192]{3,4,2,1,0:T(8,128)(2,1)}, bf16[4,2,3,128,192]{3,4,2,1,0:T(8,128)(2,1)}, u32[]{:S(2)}, u32[]{:S(2)}) collective-permute-start(bf16[4,2,3,128,192]{3,4,2,1,0:T(8,128)(2,1)} %copy.83), channel_id=1, source_target_pairs={{0,31},{16,0},{1,16},{17,1},{2,17},{18,2},{3,18},{19,3},{4,19},{20... | collective-permute-start | bytes 3538952 | tf_op jit(solution)/shard_map/ppermute | solution.py:696
  127.2 3.9 copy-start.17
  127.2 3.9 copy-start.16
  127.2 3.9 copy-start.15
  129.8 52.8 %collective-permute-start.6 = (bf16[4,2,3,128,192]{3,4,2,1,0:T(8,128)(2,1)}, bf16[4,2,3,128,192]{3,4,2,1,0:T(8,128)(2,1)}, u32[]{:S(2)}, u32[]{:S(2)}) collective-permute-start(bf16[4,2,3,128,192]{3,4,2,1,0:T(8,128)(2,1)} %copy.77), channel_id=1, source_target_pairs={{0,31},{16,0},{1,16},{17,1},{2,17},{18,2},{3,18},{19,3},{4,19},{20... | collective-permute-start | bytes 3538952 | tf_op jit(solution)/shard_map/ppermute | solution.py:696
  134.9 1.2 copy-start
  174.7 96.5 %collective-permute-start.2 = (bf16[4,2,3,128,192]{3,4,2,1,0:T(8,128)(2,1)}, bf16[4,2,3,128,192]{3,4,2,1,0:T(8,128)(2,1)}, u32[]{:S(2)}, u32[]{:S(2)}) collective-permute-start(bf16[4,2,3,128,192]{3,4,2,1,0:T(8,128)(2,1)} %copy.74), channel_id=1, source_target_pairs={{0,16},{16,1},{1,17},{17,2},{2,18},{18,3},{3,19},{19,4},{4,20},{20... | collective-permute-start | bytes 3538952 | tf_op jit(solution)/shard_map/ppermute | solution.py:707
  174.9 221.9 %collective-permute-start.5 = (f32[4,16,32,192]{3,2,1,0:T(8,128)}, f32[4,16,32,192]{3,2,1,0:T(8,128)}, u32[]{:S(2)}, u32[]{:S(2)}) collective-permute-start(f32[4,16,32,192]{3,2,1,0:T(8,128)} %get-tuple-element.107), channel_id=1, source_target_pairs={{0,16},{1,17},{2,18},{3,19},{4,20},{5,21},{6,22},{7,23},{8,24},{9,... | collective-permute-start | bytes 4718600 | tf_op jit(solution)/shard_map/ppermute | solution.py:710
  221.9 41.2 %copy-start.18 = (s32[4096]{0:T(1024)S(1)}, s32[4096]{0:T(1024)}, u32[]{:S(2)}) copy-start(s32[4096]{0:T(1024)} %constant.44.clone) | copy-start | bytes 49156
  258.9 6.7 %copy-start.12 = (f32[192,768]{1,0:T(8,128)S(1)}, f32[192,768]{1,0:T(8,128)}, u32[]{:S(2)}) copy-start(f32[192,768]{1,0:T(8,128)} %get-tuple-element.167) | copy-start | bytes 1769476
  260.8 4.9 copy-start.10
  270.8 19.5 %collective-permute-start.7 = (bf16[4,2,3,128,192]{3,4,2,1,0:T(8,128)(2,1)}, bf16[4,2,3,128,192]{3,4,2,1,0:T(8,128)(2,1)}, u32[]{:S(2)}, u32[]{:S(2)}) collective-permute-start(bf16[4,2,3,128,192]{3,4,2,1,0:T(8,128)(2,1)} %copy.80), channel_id=1, source_target_pairs={{0,16},{16,1},{1,17},{17,2},{2,18},{18,3},{3,19},{19,4},{4,20},{20... | collective-permute-start | bytes 3538952 | tf_op jit(solution)/shard_map/ppermute | solution.py:707
  270.8 68.9 %collective-permute-start.12 = (bf16[4,2,3,128,192]{3,4,2,1,0:T(8,128)(2,1)}, bf16[4,2,3,128,192]{3,4,2,1,0:T(8,128)(2,1)}, u32[]{:S(2)}, u32[]{:S(2)}) collective-permute-start(bf16[4,2,3,128,192]{3,4,2,1,0:T(8,128)(2,1)} %copy.86), channel_id=1, source_target_pairs={{0,16},{16,1},{1,17},{17,2},{2,18},{18,3},{3,19},{19,4},{4,20},{20... | collective-permute-start | bytes 3538952 | tf_op jit(solution)/shard_map/ppermute | solution.py:707
  366.2 7.4 %copy-start.11 = (f32[192,768]{1,0:T(8,128)S(1)}, f32[192,768]{1,0:T(8,128)}, u32[]{:S(2)}) copy-start(f32[192,768]{1,0:T(8,128)} %get-tuple-element.161) | copy-start | bytes 1769476
  375.6 0.9 copy-start.9
  375.6 1.0 copy-start.8
  376.6 1.7 copy-start.1
  376.6 2.1 copy-start.3
  378.8 21.6 %collective-permute-start.16 = (f32[390666]{0:T(1024)}, f32[390666]{0:T(1024)}, u32[]{:S(2)}, u32[]{:S(2)}) collective-permute-start(f32[390666]{0:T(1024)} %broadcast_select_fusion), channel_id=1, source_target_pairs={{0,16},{16,0},{1,17},{17,1},{2,18},{18,2},{3,19},{19,3},{4,20},{20... | collective-permute-start | bytes 4688000 | tf_op jit(solution)/shard_map/ppermute | solution.py:753
  381.5 13.6 %collective-permute-start.4 = (f32[2,16,32,192]{3,2,1,0:T(8,128)}, f32[2,16,32,192]{3,2,1,0:T(8,128)}, u32[]{:S(2)}, u32[]{:S(2)}) collective-permute-start(f32[2,16,32,192]{3,2,1,0:T(8,128)} %get-tuple-element.172), channel_id=1, source_target_pairs={{16,17},{17,18},{18,19},{19,20},{20,21},{21,22},{22,23},{23,24},{2... | collective-permute-start | bytes 2359304 | tf_op jit(solution)/shard_map/ppermute | solution.py:709
  383.3 9.1 %collective-permute-start.17 = (f32[79872]{0:T(1024)S(1)}, f32[79872]{0:T(1024)S(1)}, u32[]{:S(2)}, u32[]{:S(2)}) collective-permute-start(f32[79872]{0:T(1024)S(1)} %reshape.321), channel_id=1, source_target_pairs={{0,16},{16,0},{1,17},{17,1},{2,18},{18,2},{3,19},{19,3},{4,20},{20... | collective-permute-start | bytes 958472 | tf_op jit(solution)/shard_map/ppermute | solution.py:755
  384.2 2.2 copy-start.7
  386.4 18.3 %collective-permute-start.15 = (f32[4,16,32,192]{3,2,1,0:T(8,128)S(1)}, f32[4,16,32,192]{3,2,1,0:T(8,128)}, u32[]{:S(2)}, u32[]{:S(2)}) collective-permute-start(f32[4,16,32,192]{3,2,1,0:T(8,128)S(1)} %copy-done.7), channel_id=1, source_target_pairs={{0,16},{1,17},{2,18},{3,19},{4,20},{5,21},{6,22},{7,23},{8,24},{9,... | collective-permute-start | bytes 4718600 | tf_op jit(solution)/shard_map/ppermute | solution.py:710
  392.4 16.4 %collective-permute-start.10 = (f32[4,16,32,192]{3,2,1,0:T(8,128)}, f32[4,16,32,192]{3,2,1,0:T(8,128)}, u32[]{:S(2)}, u32[]{:S(2)}) collective-permute-start(f32[4,16,32,192]{3,2,1,0:T(8,128)} %get-tuple-element.133), channel_id=1, source_target_pairs={{0,16},{1,17},{2,18},{3,19},{4,20},{5,21},{6,22},{7,23},{8,24},{9,... | collective-permute-start | bytes 4718600 | tf_op jit(solution)/shard_map/ppermute | solution.py:710
  395.1 8.2 %collective-permute-start.14 = (f32[2,16,32,192]{3,2,1,0:T(8,128)S(1)}, f32[2,16,32,192]{3,2,1,0:T(8,128)}, u32[]{:S(2)}, u32[]{:S(2)}) collective-permute-start(f32[2,16,32,192]{3,2,1,0:T(8,128)S(1)} %get-tuple-element.176), channel_id=1, source_target_pairs={{16,17},{17,18},{18,19},{19,20},{20,21},{21,22},{22,23},{23,24},{2... | collective-permute-start | bytes 2359304 | tf_op jit(solution)/shard_map/ppermute | solution.py:709
  396.8 12.0 %collective-permute-start.9 = (f32[2,16,32,192]{3,2,1,0:T(8,128)}, f32[2,16,32,192]{3,2,1,0:T(8,128)}, u32[]{:S(2)}, u32[]{:S(2)}) collective-permute-start(f32[2,16,32,192]{3,2,1,0:T(8,128)} %get-tuple-element.174), channel_id=1, source_target_pairs={{16,17},{17,18},{18,19},{19,20},{20,21},{21,22},{22,23},{23,24},{2... | collective-permute-start | bytes 2359304 | tf_op jit(solution)/shard_map/ppermute | solution.py:709
  398.4 3.3 copy-start.2
  398.4 3.3 copy-start.4
  400.4 15.9 %collective-permute-start.3 = (f32[4,16,32,192]{3,2,1,0:T(8,128)}, f32[4,16,32,192]{3,2,1,0:T(8,128)}, u32[]{:S(2)}, u32[]{:S(2)}) collective-permute-start(f32[4,16,32,192]{3,2,1,0:T(8,128)} %get-tuple-element.106), channel_id=1, source_target_pairs={{16,0},{17,1},{18,2},{19,3},{20,4},{21,5},{22,6},{23,7},{24,8},{25... | collective-permute-start | bytes 4718600 | tf_op jit(solution)/shard_map/ppermute | solution.py:718
  403.4 22.6 %collective-permute-start.13 = (f32[4,16,32,192]{3,2,1,0:T(8,128)}, f32[4,16,32,192]{3,2,1,0:T(8,128)}, u32[]{:S(2)}, u32[]{:S(2)}) collective-permute-start(f32[4,16,32,192]{3,2,1,0:T(8,128)} %get-tuple-element.158), channel_id=1, source_target_pairs={{16,0},{17,1},{18,2},{19,3},{20,4},{21,5},{22,6},{23,7},{24,8},{25... | collective-permute-start | bytes 4718600 | tf_op jit(solution)/shard_map/ppermute | solution.py:718
  404.7 26.4 %collective-permute-start.8 = (f32[4,16,32,192]{3,2,1,0:T(8,128)}, f32[4,16,32,192]{3,2,1,0:T(8,128)}, u32[]{:S(2)}, u32[]{:S(2)}) collective-permute-start(f32[4,16,32,192]{3,2,1,0:T(8,128)} %get-tuple-element.132), channel_id=1, source_target_pairs={{16,0},{17,1},{18,2},{19,3},{20,4},{21,5},{22,6},{23,7},{24,8},{25... | collective-permute-start | bytes 4718600 | tf_op jit(solution)/shard_map/ppermute | solution.py:718
  414.1 2.2 copy-start.6
  546.5 7.3 %copy-start.5 = (f32[470538]{0:T(1024)S(1)}, f32[470538]{0:T(1024)}, u32[]{:S(2)}) copy-start(f32[470538]{0:T(1024)} %all-reduce.8.cloned.1.call-done) | copy-start | bytes 5646460
Sparse Core Ops, SparseCore 0:
  407.9 138.5 all-reduce.7
